TPU v7x, 256 devices: a whole 4x4x8 slice. The times are simulated.
256 devices in a mesh: frame: 32 (over x_hi, z, core), head: 8 (over x_lo, y).
Axes of the slice: x: 4 (x_hi: 2, x_lo: 2; x = x_hi * 2 + x_lo), y: 4, z: 8, core: 2. Of those that a mesh axis runs over, the one named last changes fastest.
Arguments:
- queries: bfloat16 [40960, 3072], P(('frame', 'head')), may hold values from -16 to 16
- keys: bfloat16 [40960, 3072], P(('frame', 'head')), may hold values from -16 to 16
- values: bfloat16 [40960, 3072], P(('frame', 'head')), may hold values from -6 to 6
- head_reach: int32 [24, 3], replicated, may hold values from 0 to 1, as said below
- frame_valid: int32 [32], replicated, may hold values from 0 to 1, as said below
Outputs:
- attended: bfloat16 [40960, 3072], P(('frame', 'head'))
Inputs may be any that keep to these rules, and one draw needn't show every extreme that they name: `head_reach`: column 0 is a time reach in frames and takes every value 0 to 1 on some head; columns 1 and 2 are tile reaches and take both 0 and 1 on some head. `frame_valid`: 1 on a leading run of at least half of the 32 frames and 0 after it; the last frame is always 0.
All inputs are finite; a program needn't handle non-finite values.
Results may differ from a plain program's by a relative error of at most 0.006.
Values may be sent and summed in bfloat16 or wider, within the bound.
A program may use at most 128 MiB of HBM per device.

v0:
```python
import jax
import jax.numpy as jnp
from jax import lax
from jax.sharding import PartitionSpec as P

DH = 128
TILE = 8
TH_TILES = 2
TW_TILES = 10
FR_DEV = 1
TREACH = 1


def with_halo(block, sides, width):
    for axis, dim in sides:
        count = lax.axis_size(axis)
        forward = [(i, i + 1) for i in range(count - 1)]
        backward = [(target, source) for source, target in forward]
        low = lax.ppermute(
            lax.slice_in_dim(block, block.shape[dim] - width, None, axis=dim), axis, forward
        )
        high = lax.ppermute(lax.slice_in_dim(block, 0, width, axis=dim), axis, backward)
        block = jnp.concatenate([low, block, high], axis=dim)
    return block


def window_mask(reach, live, pos):
    row_width = TW_TILES * TILE
    tile_y = pos // row_width // TILE
    tile_x = pos % row_width // TILE

    def bounds(tile, span_reach, count):
        size = jnp.minimum(2 * span_reach + 1, count)
        start = jnp.clip(tile - span_reach, 0, count - size)
        return (start, start + size)

    low_y, high_y = bounds(tile_y, reach[1], TH_TILES)
    low_x, high_x = bounds(tile_x, reach[2], TW_TILES)
    spatial = (tile_y[None, :] >= low_y[:, None]) & (tile_y[None, :] < high_y[:, None])
    spatial = spatial & (tile_x[None, :] >= low_x[:, None]) & (tile_x[None, :] < high_x[:, None])
    offsets = jnp.arange(2 * TREACH + 1) - TREACH
    timely = (jnp.abs(offsets) <= reach[0]) & (live > 0)
    joined = timely[None, :, None] & spatial[:, None, :]
    return joined.reshape(pos.shape[0], -1)


def attend(query_local, pair_ext, reach_rows, live_ext, keep_rows):
    frame_tokens = TH_TILES * TW_TILES * TILE * TILE
    span = 2 * TREACH + 1
    scale = DH ** (-0.5)
    local_heads = reach_rows.shape[0]
    pos = jnp.arange(frame_tokens)
    output = jnp.zeros((FR_DEV * frame_tokens, local_heads * DH), jnp.bfloat16)

    def block(number, output):
        head = number // FR_DEV
        frame = number % FR_DEV
        query = lax.dynamic_slice(
            query_local, (frame, 0, head * DH), (1, frame_tokens, DH)
        ).reshape(frame_tokens, DH)
        near = lax.dynamic_slice(pair_ext, (0, frame, 0, head * DH), (2, span, frame_tokens, DH))
        near = near.reshape(2, span * frame_tokens, DH)
        mask = window_mask(reach_rows[head], live_ext, pos)
        scores = (
            lax.dot_general(
                query, near[0], (((1,), (1,)), ((), ())), preferred_element_type=jnp.float32
            )
            * scale
        )
        scores = jnp.where(mask, scores, jnp.float32(-1e30))
        top = jnp.max(scores, axis=1, keepdims=True)
        weights = jnp.where(mask, jnp.exp(scores - top), jnp.float32(0.0)).astype(jnp.bfloat16)
        total = jnp.sum(weights.astype(jnp.float32), axis=1, keepdims=True)
        mixed = jnp.dot(weights, near[1], preferred_element_type=jnp.float32) / total
        keep = keep_rows[frame] > 0
        result = jnp.where(keep, mixed, jnp.float32(0.0)).astype(jnp.bfloat16)
        return lax.dynamic_update_slice(output, result, (frame * frame_tokens, head * DH))

    return lax.fori_loop(0, local_heads * FR_DEV, block, output)


def body(queries, keys, values, head_reach, frame_valid):
    frame_tokens = TH_TILES * TW_TILES * TILE * TILE
    total_frames = frame_valid.shape[0]
    moved = lax.all_to_all(
        jnp.stack([queries, keys, values]), "head", split_axis=2, concat_axis=1, tiled=True
    )
    query_local = moved[0].reshape(FR_DEV, frame_tokens, -1)
    own = moved[1:3].reshape(2, FR_DEV, frame_tokens, -1)
    pair_ext = with_halo(own, (("frame", 1),), TREACH)
    local_heads = query_local.shape[2] // DH
    reach_rows = lax.dynamic_slice(
        head_reach, (lax.axis_index("head") * local_heads, 0), (local_heads, 3)
    )
    first = lax.axis_index("frame") * FR_DEV - TREACH
    global_frames = first + jnp.arange(FR_DEV + 2 * TREACH)
    matches = (global_frames[:, None] == jnp.arange(total_frames)[None, :]).astype(jnp.int32)
    live_ext = jnp.sum(matches * frame_valid[None, :], axis=1)
    keep_rows = live_ext[TREACH : TREACH + FR_DEV]
    attended = attend(query_local, pair_ext, reach_rows, live_ext, keep_rows)
    return lax.all_to_all(attended, "head", split_axis=0, concat_axis=1, tiled=True)


def solution(mesh):
    placed = (
        P(("frame", "head"), None),
        P(("frame", "head"), None),
        P(("frame", "head"), None),
        P(),
        P(),
    )
    return jax.shard_map(
        body, mesh=mesh, in_specs=placed, out_specs=P(("frame", "head"), None), check_vma=False
    )
```

profile of v0, /device:TPU:4, one launch (start us, length us, event | category | flops | bytes accessed | tf_op | source)
XLA Modules:
  0.0 254.6 jit_solution(15030894898297076915)
XLA Ops:
  2.1 6.9 %copy.28 = bf16[3,160,3072]{1,0,2:T(4,128)(2,1)} copy(bf16[3,160,3072]{2,1,0:T(8,128)(2,1)S(1)} %pad_maximum_fusion.1) | data formatting | bytes 5898240 | tf_op jit(solution)/shard_map/stack | solution.py:86
  9.1 9.3 %reshape.374 = bf16[8,2,92160]{2,1,0:T(2,128)(2,1)S(1)} reshape(bf16[3072,3,160]{2,1,0:T(4,128)(2,1)} %bitcast.53) | data formatting | bytes 5898240
  18.4 41.6 %all_to_all.34 = bf16[8,2,92160]{2,1,0:T(2,128)(2,1)} all-to-all(bf16[8,2,92160]{2,1,0:T(2,128)(2,1)S(1)} %reshape.374), channel_id=1, replica_groups=mesh['frame'=32,'head'=8] {'head'}, dimensions={0} | all-to-all | bytes 5898240 | tf_op jit(solution)/shard_map/all_to_all | solution.py:85
  60.0 10.5 %reshape.375 = bf16[3072,3,160]{2,1,0:T(4,128)(2,1)} reshape(bf16[8,2,92160]{2,1,0:T(2,128)(2,1)} %all_to_all.34) | data formatting | bytes 5898240
  70.5 6.2 %slice.88 = bf16[2,8,160,384]{2,0,3,1:T(2,128)(2,1)S(1)} slice(bf16[3,8,160,384]{2,0,3,1:T(4,128)(2,1)} %bitcast.51), slice={[1:3], [0:8], [0:160], [0:384]} | slice | bytes 3932160 | tf_op jit(solution)/shard_map/slice | solution.py:89
  76.6 5.4 %copy.30 = bf16[2,8,160,384]{3,2,1,0:T(8,128)(2,1)} copy(bf16[2,8,160,384]{2,0,3,1:T(2,128)(2,1)S(1)} %slice.88) | data formatting | bytes 3932160 | tf_op jit(solution)/shard_map/slice | solution.py:89
  82.0 5.8 %collective-permute-start.1 = (bf16[2,1,1280,384]{3,2,1,0:T(8,128)(2,1)}, bf16[2,1,1280,384]{3,2,1,0:T(8,128)(2,1)}, u32[]{:S(2)}, u32[]{:S(2)}) collective-permute-start(bf16[2,1,1280,384]{3,2,1,0:T(8,128)(2,1)} %bitcast.55), channel_id=1, source_target_pairs={{8,0},{16,8},{24,16},{32,24},{40,32},{48,40},{56,48},{64,56},{72,6... | collective-permute-start | bytes 5898248 | tf_op jit(solution)/shard_map/ppermute | solution.py:22
  91.4 4.9 %slice.87 = bf16[1,8,160,384]{2,0,3,1:T(2,128)(2,1)S(1)} slice(bf16[3,8,160,384]{2,0,3,1:T(4,128)(2,1)} %bitcast.52), slice={[0:1], [0:8], [0:160], [0:384]} | slice | bytes 1966080 | tf_op jit(solution)/shard_map/slice | solution.py:88
  96.3 4.9 %copy.29 = bf16[1,8,160,384]{3,2,1,0:T(8,128)(2,1)} copy(bf16[1,8,160,384]{2,0,3,1:T(2,128)(2,1)S(1)} %slice.87) | data formatting | bytes 1966080 | tf_op jit(solution)/shard_map/slice | solution.py:88
  101.2 9.0 %collective-permute-done.1 = bf16[2,1,1280,384]{3,2,1,0:T(8,128)(2,1)} collective-permute-done((bf16[2,1,1280,384]{3,2,1,0:T(8,128)(2,1)}, bf16[2,1,1280,384]{3,2,1,0:T(8,128)(2,1)}, u32[]{:S(2)}, u32[]{:S(2)}) %collective-permute-start.1) | collective-permute-done | bytes 1966112 | tf_op jit(solution)/shard_map/ppermute | solution.py:22
  110.3 7.4 %collective-permute-done = bf16[2,1,1280,384]{3,2,1,0:T(8,128)(2,1)} collective-permute-done((bf16[2,1,1280,384]{3,2,1,0:T(8,128)(2,1)}, bf16[2,1,1280,384]{3,2,1,0:T(8,128)(2,1)}, u32[]{:S(2)}, u32[]{:S(2)}) %collective-permute-start) | collective-permute-done | bytes 1966112 | tf_op jit(solution)/shard_map/ppermute | solution.py:19
  117.7 6.2 %pad_maximum_fusion = bf16[2,3,1280,384]{3,2,1,0:T(8,128)(2,1)} fusion(bf16[2,1,1280,384]{3,2,1,0:T(8,128)(2,1)} %collective-permute-done.1, bf16[2,1,1280,384]{3,2,1,0:T(8,128)(2,1)} %bitcast.57, bf16[2,1,1280,384]{3,2,1,0:T(8,128)(2,1)} %collective-permute-done), kind=kLoop, calls=%fused_computation.60 | loop fusion | flops 5898240 | bytes 11796480 | tf_op jit(solution)/shard_map/concatenate | solution.py:23
  125.0 113.7 %while.18 = (s32[]{:T(128)}, bf16[1280,384]{1,0:T(8,128)(2,1)}, pred[]{:T(512)}, s32[3,3]{1,0:T(4,128)S(1)}, s32[3]{0:T(128)S(1)}, /*index=5*/bf16[1,1280,384]{2...) while((s32[]{:T(128)}, bf16[1280,384]{1,0:T(8,128)(2,1)}, ...), condition=%wide.region_4.5_spmd.clone.clone, body=%wide.region_1.4_spmd.clone.clone.sunk | while | flops 2577812480 | bytes 113156792 | solution.py:79
  128.9 2.5 compare_and_fusion.4
  133.0 3.5 %and.426 = pred[1280,3,1280]{0,2,1:T(32,128)(4,1)} broadcast(pred[1280,1280]{0,1:T(8,128)(4,1)S(1)} %compare_and_fusion.4), dimensions={0,2} | broadcast | bytes 6553600 | tf_op jit(solution)/shard_map/while/body/eval_jaxpr/and | solution.py:43
  136.6 9.8 %copy.35 = pred[1280,3840]{1,0:T(32,128)(4,1)} copy(pred[1280,3840]{0,1:T(32,128)(4,1)} %bitcast.49) | data formatting | bytes 9830400 | tf_op jit(solution)/shard_map/while/body/eval_jaxpr/and | solution.py:43
  146.4 6.4 %fusion.47 = (f32[1280]{0:T(1024)S(1)}, f32[1280,3840]{1,0:T(8,128)S(1)}) fusion(bf16[3840,128]{1,0:T(8,128)(2,1)S(1)} %bitcast.50, bf16[1,1280,384]{2,1,0:T(8,128)(2,1)} %get-tuple-element.469, s32[]{:T(128)S(6)} %select_n.377, pred[1280,3840]{1,0:T(32,128)(4,1)} %copy.35, pred[3840]{0:T(1024)(128)(4,1)S(1)} %and.428), kind=kOutput, calls=%fused_computation.67.clone.1 | convolution fusion | flops 1277950720 | bytes 25895684 | tf_op jit(solution)/shard_map/while/body/eval_jaxpr/dot_general | solution.py:65
  152.8 6.6 %convert_reduce_fusion.2 = (f32[1280]{0:T(1024)S(1)}, bf16[1280,3840]{1,0:T(8,128)(2,1)S(1)}) fusion(f32[1280,3840]{1,0:T(8,128)S(1)} %get-tuple-element.431, f32[1280]{0:T(1024)S(1)} %get-tuple-element.432, pred[1280,3840]{1,0:T(32,128)(4,1)S(1)} %copy-done.2, pred[3840]{0:T(1024)(128)(4,1)S(1)} %and.428), kind=kLoop, calls=%fused_computation.3.clone.1 | loop fusion | flops 29489920 | bytes 34420480 | tf_op jit(solution)/shard_map/while/body/eval_jaxpr/reduce_sum | solution.py:73
  159.4 3.5 %fusion.48 = bf16[1280,384]{1,0:T(8,128)(2,1)} fusion(bf16[1280,384]{1,0:T(8,128)(2,1)} %get-tuple-element.451, s32[]{:T(128)S(6)} %select_n.377, bf16[1280,3840]{1,0:T(8,128)(2,1)S(1)} %get-tuple-element.433, bf16[3840,128]{1,0:T(8,128)(2,1)S(1)} %bitcast.54, f32[1280]{0:T(1024)S(1)} %get-tuple-element.435, pred[]{:T(512)} %get-tuple-element.466), kind=kOutput, calls=%fused_computation.10.clone.1 | convolution fusion | flops 1258782720 | bytes 11146756 | tf_op jit(solution)/shard_map/while/body/eval_jaxpr/dot_general | solution.py:74
  166.8 2.5 compare_and_fusion.4
  171.0 3.5 %and.426 = pred[1280,3,1280]{0,2,1:T(32,128)(4,1)} broadcast(pred[1280,1280]{0,1:T(8,128)(4,1)S(1)} %compare_and_fusion.4), dimensions={0,2} | broadcast | bytes 6553600 | tf_op jit(solution)/shard_map/while/body/eval_jaxpr/and | solution.py:43
  174.5 9.8 %copy.35 = pred[1280,3840]{1,0:T(32,128)(4,1)} copy(pred[1280,3840]{0,1:T(32,128)(4,1)} %bitcast.49) | data formatting | bytes 9830400 | tf_op jit(solution)/shard_map/while/body/eval_jaxpr/and | solution.py:43
  184.3 6.4 %fusion.47 = (f32[1280]{0:T(1024)S(1)}, f32[1280,3840]{1,0:T(8,128)S(1)}) fusion(bf16[3840,128]{1,0:T(8,128)(2,1)S(1)} %bitcast.50, bf16[1,1280,384]{2,1,0:T(8,128)(2,1)} %get-tuple-element.469, s32[]{:T(128)S(6)} %select_n.377, pred[1280,3840]{1,0:T(32,128)(4,1)} %copy.35, pred[3840]{0:T(1024)(128)(4,1)S(1)} %and.428), kind=kOutput, calls=%fused_computation.67.clone.1 | convolution fusion | flops 1277950720 | bytes 25895684 | tf_op jit(solution)/shard_map/while/body/eval_jaxpr/dot_general | solution.py:65
  190.7 6.6 %convert_reduce_fusion.2 = (f32[1280]{0:T(1024)S(1)}, bf16[1280,3840]{1,0:T(8,128)(2,1)S(1)}) fusion(f32[1280,3840]{1,0:T(8,128)S(1)} %get-tuple-element.431, f32[1280]{0:T(1024)S(1)} %get-tuple-element.432, pred[1280,3840]{1,0:T(32,128)(4,1)S(1)} %copy-done.2, pred[3840]{0:T(1024)(128)(4,1)S(1)} %and.428), kind=kLoop, calls=%fused_computation.3.clone.1 | loop fusion | flops 29489920 | bytes 34420480 | tf_op jit(solution)/shard_map/while/body/eval_jaxpr/reduce_sum | solution.py:73
  197.3 3.5 %fusion.48 = bf16[1280,384]{1,0:T(8,128)(2,1)} fusion(bf16[1280,384]{1,0:T(8,128)(2,1)} %get-tuple-element.451, s32[]{:T(128)S(6)} %select_n.377, bf16[1280,3840]{1,0:T(8,128)(2,1)S(1)} %get-tuple-element.433, bf16[3840,128]{1,0:T(8,128)(2,1)S(1)} %bitcast.54, f32[1280]{0:T(1024)S(1)} %get-tuple-element.435, pred[]{:T(512)} %get-tuple-element.466), kind=kOutput, calls=%fused_computation.10.clone.1 | convolution fusion | flops 1258782720 | bytes 11146756 | tf_op jit(solution)/shard_map/while/body/eval_jaxpr/dot_general | solution.py:74
  204.7 2.5 compare_and_fusion.4
  208.9 3.5 %and.426 = pred[1280,3,1280]{0,2,1:T(32,128)(4,1)} broadcast(pred[1280,1280]{0,1:T(8,128)(4,1)S(1)} %compare_and_fusion.4), dimensions={0,2} | broadcast | bytes 6553600 | tf_op jit(solution)/shard_map/while/body/eval_jaxpr/and | solution.py:43
  212.4 9.8 %copy.35 = pred[1280,3840]{1,0:T(32,128)(4,1)} copy(pred[1280,3840]{0,1:T(32,128)(4,1)} %bitcast.49) | data formatting | bytes 9830400 | tf_op jit(solution)/shard_map/while/body/eval_jaxpr/and | solution.py:43
  222.2 6.4 %fusion.47 = (f32[1280]{0:T(1024)S(1)}, f32[1280,3840]{1,0:T(8,128)S(1)}) fusion(bf16[3840,128]{1,0:T(8,128)(2,1)S(1)} %bitcast.50, bf16[1,1280,384]{2,1,0:T(8,128)(2,1)} %get-tuple-element.469, s32[]{:T(128)S(6)} %select_n.377, pred[1280,3840]{1,0:T(32,128)(4,1)} %copy.35, pred[3840]{0:T(1024)(128)(4,1)S(1)} %and.428), kind=kOutput, calls=%fused_computation.67.clone.1 | convolution fusion | flops 1277950720 | bytes 25895684 | tf_op jit(solution)/shard_map/while/body/eval_jaxpr/dot_general | solution.py:65
  228.6 6.6 %convert_reduce_fusion.2 = (f32[1280]{0:T(1024)S(1)}, bf16[1280,3840]{1,0:T(8,128)(2,1)S(1)}) fusion(f32[1280,3840]{1,0:T(8,128)S(1)} %get-tuple-element.431, f32[1280]{0:T(1024)S(1)} %get-tuple-element.432, pred[1280,3840]{1,0:T(32,128)(4,1)S(1)} %copy-done.2, pred[3840]{0:T(1024)(128)(4,1)S(1)} %and.428), kind=kLoop, calls=%fused_computation.3.clone.1 | loop fusion | flops 29489920 | bytes 34420480 | tf_op jit(solution)/shard_map/while/body/eval_jaxpr/reduce_sum | solution.py:73
  235.2 3.5 %fusion.48 = bf16[1280,384]{1,0:T(8,128)(2,1)} fusion(bf16[1280,384]{1,0:T(8,128)(2,1)} %get-tuple-element.451, s32[]{:T(128)S(6)} %select_n.377, bf16[1280,3840]{1,0:T(8,128)(2,1)S(1)} %get-tuple-element.433, bf16[3840,128]{1,0:T(8,128)(2,1)S(1)} %bitcast.54, f32[1280]{0:T(1024)S(1)} %get-tuple-element.435, pred[]{:T(512)} %get-tuple-element.466), kind=kOutput, calls=%fused_computation.10.clone.1 | convolution fusion | flops 1258782720 | bytes 11146756 | tf_op jit(solution)/shard_map/while/body/eval_jaxpr/dot_general | solution.py:74
  238.7 14.7 %all_to_all.35 = bf16[8,160,384]{2,1,0:T(8,128)(2,1)S(1)} all-to-all(bf16[8,160,384]{2,1,0:T(8,128)(2,1)} %bitcast.59), channel_id=1, replica_groups=mesh['frame'=32,'head'=8] {'head'}, dimensions={0} | all-to-all | bytes 1966080 | tf_op jit(solution)/shard_map/all_to_all | solution.py:101
  (54 shorter events, 20.2 us)
Async XLA Ops:
  0.0 90.5 %copy-start = (s32[24,3]{0,1:T(4,128)S(1)}, s32[24,3]{0,1:T(4,128)}, u32[]{:S(2)}) copy-start(s32[24,3]{0,1:T(4,128)} %param.10) | copy-start | bytes 868
  70.5 19.3 %copy-start.3 = (s32[32]{0:T(128)S(1)}, s32[32]{0:T(128)}, u32[]{:S(2)}) copy-start(s32[32]{0:T(128)} %param.11) | copy-start | bytes 388
  82.0 28.2 %collective-permute-start.1 = (bf16[2,1,1280,384]{3,2,1,0:T(8,128)(2,1)}, bf16[2,1,1280,384]{3,2,1,0:T(8,128)(2,1)}, u32[]{:S(2)}, u32[]{:S(2)}) collective-permute-start(bf16[2,1,1280,384]{3,2,1,0:T(8,128)(2,1)} %bitcast.55), channel_id=1, source_target_pairs={{8,0},{16,8},{24,16},{32,24},{40,32},{48,40},{56,48},{64,56},{72,6... | collective-permute-start | bytes 5898248 | tf_op jit(solution)/shard_map/ppermute | solution.py:22
  87.8 29.9 %collective-permute-start = (bf16[2,1,1280,384]{3,2,1,0:T(8,128)(2,1)}, bf16[2,1,1280,384]{3,2,1,0:T(8,128)(2,1)}, u32[]{:S(2)}, u32[]{:S(2)}) collective-permute-start(bf16[2,1,1280,384]{3,2,1,0:T(8,128)(2,1)} %bitcast.56), channel_id=1, source_target_pairs={{0,8},{8,16},{16,24},{24,32},{32,40},{40,48},{48,56},{56,64},{64,7... | collective-permute-start | bytes 5898248 | tf_op jit(solution)/shard_map/ppermute | solution.py:19
  146.4 6.5 %copy-start.2 = (pred[1280,3840]{1,0:T(32,128)(4,1)S(1)}, pred[1280,3840]{1,0:T(32,128)(4,1)}, u32[]{:S(2)}) copy-start(pred[1280,3840]{1,0:T(32,128)(4,1)} %copy.35) | copy-start | bytes 14745604 | tf_op jit(solution)/shard_map/while
  184.3 6.5 %copy-start.2 = (pred[1280,3840]{1,0:T(32,128)(4,1)S(1)}, pred[1280,3840]{1,0:T(32,128)(4,1)}, u32[]{:S(2)}) copy-start(pred[1280,3840]{1,0:T(32,128)(4,1)} %copy.35) | copy-start | bytes 14745604 | tf_op jit(solution)/shard_map/while
  222.2 6.5 %copy-start.2 = (pred[1280,3840]{1,0:T(32,128)(4,1)S(1)}, pred[1280,3840]{1,0:T(32,128)(4,1)}, u32[]{:S(2)}) copy-start(pred[1280,3840]{1,0:T(32,128)(4,1)} %copy.35) | copy-start | bytes 14745604 | tf_op jit(solution)/shard_map/while
  238.7 15.9 %copy-start.1 = (s32[24,3]{0,1:T(4,128)S(1)}, s32[24,3]{0,1:T(4,128)}, u32[]{:S(2)}) copy-start(s32[24,3]{0,1:T(4,128)} %param.10) | copy-start | bytes 868
where the time goes:
time: 256 us; the launch traced here: 255 us
  local copies, waits for them, and re-layouts  98 us (38%)
  blocking collectives  56.4 us (22%)
  other arithmetic  41.9 us (16%)
  matrix products  29.7 us (12%)
  waiting for transfers between devices  16.5 us (6%)
  starting transfers between devices  7.69 us (3%)
  loops' own time  3.67 us (1%)
    all_to_all x1, blocking collectives, body(): lax.all_to_all(jnp.stack([queries, keys, values]), 'head', split_axis=2,...  41.6 us
    and x12, local copies, waits for them, and re-layouts, window_mask(): joined = timely[None, :, None] & spatial[:, None, :]  40.2 us
    unnamed x9, local copies, waits for them, and re-layouts  19.9 us
    reduce_sum x3, other arithmetic, block(): total = jnp.sum(weights.astype(jnp.float32), axis=1, keepdims=True)  19.7 us
    dot_general x3, matrix products, block(): lax.dot_general(query, near[0], (((1,), (1,)), ((), ())), preferred_eleme...  19.3 us
    all_to_all x1, blocking collectives, body(): lax.all_to_all(attended, 'head', split_axis=0, concat_axis=1, tiled=True)  14.7 us
    slice x2, local copies, waits for them, and re-layouts, body(): own = moved[1:3].reshape(2, FR_DEV, frame_tokens, -1)  11.6 us
    dot_general x3, matrix products, block(): jnp.dot(weights, near[1], preferred_element_type=jnp.float32) / total  10.4 us
  transfers between devices with their start and end apart: 2, of which 2 were waited for; matrix products, arithmetic and copies ran while one was open for 4% of the time, Pallas kernels for 0%

commit v1 on v0

v1 whole, which is shorter than its diff:
```python
import functools
import math

import jax
import jax.numpy as jnp
from jax import lax
from jax.experimental import pallas as pl
from jax.experimental.pallas import tpu as pltpu
from jax.sharding import PartitionSpec as P

DH = 128
ROWS = 2
PAIRS = 5
PIX = 16
TW = 10
LOCAL = 3
VMEM = 64 * 2**20
MESH = pl.DeviceIdType.MESH
BIG = float(2**20)
SCALE = math.log2(math.e) / math.sqrt(DH)


def query_features(pair, reach_h, reach_w):
    shape = (8 * ROWS * PIX, DH)
    row = lax.broadcasted_iota(jnp.int32, shape, 0)
    col = lax.broadcasted_iota(jnp.int32, shape, 1)
    tile_y = row >> 7
    tile_x = 2 * pair + ((row & 15) >> 3)
    key_y = (col >= TW).astype(jnp.int32)
    key_x = col - TW * key_y
    size_y = jnp.minimum(2 * reach_h + 1, 2)
    size_x = jnp.minimum(2 * reach_w + 1, TW)
    low_y = jnp.clip(tile_y - reach_h, 0, 2 - size_y)
    low_x = jnp.clip(tile_x - reach_w, 0, TW - size_x)
    inside = (key_y >= low_y) & (key_y < low_y + size_y)
    inside = inside & (key_x >= low_x) & (key_x < low_x + size_x)
    return jnp.where(inside, jnp.float32(0.0), jnp.float32(-BIG))


def key_features(part, pair):
    shape = (ROWS, PIX, DH)
    pix = lax.broadcasted_iota(jnp.int32, shape, 1)
    col = lax.broadcasted_iota(jnp.int32, shape, 2)
    tile = (part // 4) * TW + 2 * pair + (pix >> 3)
    return jnp.where(col == tile, jnp.float32(1.0), jnp.float32(0.0)).astype(jnp.bfloat16)


def wait_bytes(ref, sem):
    pltpu.make_async_copy(ref, ref, sem).wait()


def kernel(
    frames, reach_hbm, valid_hbm, q_ref, k_ref, v_ref, out_ref,
    qbuf, kvbuf, kfeat, obuf, reach_ref, valid_ref,
    send_sem, in_sem, fwd_sem, halo_sem, out_send_sem, out_sem, small_sem,
):
    frame = lax.axis_index("frame")
    me = lax.axis_index("head")
    half = frames // 2

    def swap(index, at):
        return lax.rem(index + jnp.where(at >= half, 4, 0), 8)

    group = swap(me, frame)
    has_prev = frame > 0
    has_next = frame < frames - 1
    prev_id = {"frame": frame - 1, "head": swap(group, frame - 1)}
    next_id = {"frame": frame + 1, "head": swap(group, frame + 1)}

    def peer(step):
        part = lax.rem(me // 4 + step // 4, 2) * 4 + lax.rem(me + step, 4)
        return part

    barrier = pltpu.get_barrier_semaphore()
    for step in range(1, 8):
        pl.semaphore_signal(
            barrier, inc=1, device_id={"frame": frame, "head": peer(step)}, device_id_type=MESH
        )

    @pl.when(has_prev)
    def _():
        pl.semaphore_signal(barrier, inc=1, device_id=prev_id, device_id_type=MESH)

    @pl.when(has_next)
    def _():
        pl.semaphore_signal(barrier, inc=1, device_id=next_id, device_id_type=MESH)

    pl.semaphore_wait(
        barrier, 7 + jnp.where(has_prev, 1, 0) + jnp.where(has_next, 1, 0)
    )

    def cols(of_group, head):
        return pl.ds(pl.multiple_of((of_group * LOCAL + head) * DH, DH), DH)

    order = (5, 1, 4, 3, 6, 2, 7)

    def send_head(head):
        for at, ref in ((1, k_ref), (2, v_ref), (0, q_ref)):
            land = qbuf.at[head, me] if at == 0 else kvbuf.at[at - 1, 1, head, me]
            for step in order:
                target = peer(step)
                pltpu.make_async_remote_copy(
                    src_ref=ref.at[:, :, :, cols(swap(target, frame), head)],
                    dst_ref=land,
                    send_sem=send_sem.at[at],
                    recv_sem=in_sem.at[at, head],
                    device_id={"frame": frame, "head": target},
                    device_id_type=MESH,
                ).start()
            pltpu.make_async_copy(
                ref.at[:, :, :, cols(group, head)], land, in_sem.at[at, head]
            ).start()

    for head in range(LOCAL):
        send_head(head)

    reach_copy = pltpu.make_async_copy(reach_hbm, reach_ref, small_sem.at[0])
    valid_copy = pltpu.make_async_copy(valid_hbm, valid_ref, small_sem.at[1])
    reach_copy.start()
    valid_copy.start()

    for part in range(8):
        for pair in range(PAIRS):
            kfeat[part, :, pair] = key_features(part, pair)

    @pl.when(jnp.logical_not(has_prev))
    def _():
        kvbuf[:, 0] = jnp.zeros(kvbuf.shape[:1] + kvbuf.shape[2:], jnp.bfloat16)

    @pl.when(jnp.logical_not(has_next))
    def _():
        kvbuf[:, 2] = jnp.zeros(kvbuf.shape[:1] + kvbuf.shape[2:], jnp.bfloat16)

    def forward(head, kv, way):
        return pltpu.make_async_remote_copy(
            src_ref=kvbuf.at[kv, 1, head],
            dst_ref=kvbuf.at[kv, 2 - 2 * way, head],
            send_sem=fwd_sem.at[kv, way, head],
            recv_sem=halo_sem.at[kv, way, head],
            device_id=(prev_id, next_id)[way],
            device_id_type=MESH,
        )

    def pass_on(head):
        for kv in range(2):
            wait_bytes(kvbuf.at[kv, 1, head], in_sem.at[kv + 1, head])

            @pl.when(has_prev)
            def _():
                forward(head, kv, 0).start()

            @pl.when(has_next)
            def _():
                forward(head, kv, 1).start()

    reach_copy.wait()
    valid_copy.wait()
    live_own = valid_ref[0, frame]
    live_prev = jnp.where(has_prev, valid_ref[0, jnp.maximum(frame - 1, 0)], 0)
    live_next = jnp.where(has_next, valid_ref[0, jnp.minimum(frame + 1, frames - 1)], 0)

    def attend(head, pair):
        row = group * LOCAL + head
        reach_t = reach_ref[0, row]
        base = query_features(pair, reach_ref[1, row], reach_ref[2, row])
        near = reach_t >= 1
        allowed = ((live_prev > 0) & near, live_own > 0, (live_next > 0) & near)
        query = qbuf[head, :, :, pair].reshape(8 * ROWS * PIX, DH)
        first, last = max(pair - 1, 0), min(pair + 2, PAIRS)
        count = 8 * ROWS * (last - first) * PIX
        tiles = kfeat[:, :, first:last].reshape(count, DH)
        scores = []
        for slot in range(3):
            features = jnp.minimum(
                base, jnp.where(allowed[slot], jnp.float32(0.0), jnp.float32(-BIG))
            ).astype(jnp.bfloat16)
            keys = kvbuf[0, slot, head, :, :, first:last].reshape(count, DH)
            scores.append(
                lax.dot_general(
                    jnp.concatenate([query, features], axis=1),
                    jnp.concatenate([keys, tiles], axis=1),
                    (((1,), (1,)), ((), ())),
                    preferred_element_type=jnp.float32,
                )
            )
        top = functools.reduce(jnp.maximum, [jnp.max(s, axis=1, keepdims=True) for s in scores])
        ones = jnp.ones((count, DH), jnp.bfloat16)
        mixed = None
        for slot in range(3):
            weights = jnp.exp2((scores[slot] - top) * SCALE).astype(jnp.bfloat16)
            values = kvbuf[1, slot, head, :, :, first:last].reshape(count, DH)
            term = jnp.dot(
                weights,
                jnp.concatenate([values, ones], axis=1),
                preferred_element_type=jnp.float32,
            )
            mixed = term if mixed is None else mixed + term
        result = mixed[:, :DH] / mixed[:, DH:]
        result = jnp.where(live_own > 0, result, jnp.float32(0.0)).astype(jnp.bfloat16)
        obuf[head, :, :, pair] = result.reshape(8, ROWS, PIX, DH)

    def send_out(head):
        for step in order:
            target = peer(step)
            pltpu.make_async_remote_copy(
                src_ref=obuf.at[head, target],
                dst_ref=out_ref.at[:, :, :, cols(group, head)],
                send_sem=out_send_sem,
                recv_sem=out_sem,
                device_id={"frame": frame, "head": target},
                device_id_type=MESH,
            ).start()
        pltpu.make_async_copy(
            obuf.at[head, me], out_ref.at[:, :, :, cols(group, head)], out_sem
        ).start()

    pass_on(0)

    def per_head(head, carry):
        @pl.when(head < LOCAL - 1)
        def _():
            pass_on(head + 1)

        wait_bytes(qbuf.at[head], in_sem.at[0, head])
        for kv in range(2):

            @pl.when(has_next)
            def _():
                forward(head, kv, 0).wait_recv()

            @pl.when(has_prev)
            def _():
                forward(head, kv, 1).wait_recv()

        for pair in range(PAIRS):
            attend(head, pair)
        send_out(head)
        return carry

    lax.fori_loop(0, LOCAL, per_head, 0)

    for at in range(3):
        wait_bytes(qbuf.at[:, 0:7], send_sem.at[at])
    for head in range(LOCAL):
        for kv in range(2):

            @pl.when(has_prev)
            def _():
                forward(head, kv, 0).wait_send()

            @pl.when(has_next)
            def _():
                forward(head, kv, 1).wait_send()

    wait_bytes(obuf.at[:, 0:7], out_send_sem)
    wait_bytes(obuf, out_sem)


def solution(mesh):
    frames = mesh.shape["frame"]
    block = (8, ROWS, PAIRS, PIX, DH)

    def body(queries, keys, values, head_reach, frame_valid):
        grid = (ROWS, PAIRS, PIX, queries.shape[1])
        hbm = pl.BlockSpec(memory_space=pltpu.HBM)
        out = pl.pallas_call(
            functools.partial(kernel, frames),
            out_shape=jax.ShapeDtypeStruct(grid, jnp.bfloat16),
            in_specs=[hbm] * 5,
            out_specs=hbm,
            scratch_shapes=[
                pltpu.VMEM((LOCAL,) + block, jnp.bfloat16),
                pltpu.VMEM((2, 3, LOCAL) + block, jnp.bfloat16),
                pltpu.VMEM(block, jnp.bfloat16),
                pltpu.VMEM((LOCAL,) + block, jnp.bfloat16),
                pltpu.SMEM((3, head_reach.shape[0]), jnp.int32),
                pltpu.SMEM((1, frames), jnp.int32),
                pltpu.SemaphoreType.DMA((3,)),
                pltpu.SemaphoreType.DMA((3, LOCAL)),
                pltpu.SemaphoreType.DMA((2, 2, LOCAL)),
                pltpu.SemaphoreType.DMA((2, 2, LOCAL)),
                pltpu.SemaphoreType.DMA,
                pltpu.SemaphoreType.DMA,
                pltpu.SemaphoreType.DMA((2,)),
            ],
            compiler_params=pltpu.CompilerParams(
                collective_id=0, has_side_effects=True, vmem_limit_bytes=VMEM
            ),
        )(
            head_reach.T,
            frame_valid.reshape(1, frames),
            queries.reshape(grid),
            keys.reshape(grid),
            values.reshape(grid),
        )
        return out.reshape(queries.shape)

    rows = P(("frame", "head"), None)
    return jax.shard_map(
        body, mesh=mesh, in_specs=(rows, rows, rows, P(), P()), out_specs=rows, check_vma=False
    )
```

time: 256 us -> 55.9 us (0.22)
  local copies, waits for them, and re-layouts: 98 us -> 2.21 us
  blocking collectives: 56.4 us -> 0 us
  Pallas kernels: 0 us -> 53.5 us
  other arithmetic: 41.9 us -> 0 us
  matrix products: 29.7 us -> 0 us
  waiting for transfers between devices: 16.5 us -> 0 us
  starting transfers between devices: 7.69 us -> 0 us
  loops' own time: 3.67 us -> 0 us
    all_to_all x2 -> x0, blocking collectives: 56.4 us -> none  [the longest x1 41.6 us: body(): lax.all_to_all(jnp.stack([queries, keys, values]), 'head', split_axis=2,...]
    pallas_call x0 -> x1, Pallas kernels: none -> 53.5 us  [body(): pl.pallas_call(functools.partial(kernel, frames), out_shape=jax.ShapeDtyp...]
    and x12 -> x0, local copies, waits for them, and re-layouts: 40.2 us -> none  [window_mask(): joined = timely[None, :, None] & spatial[:, None, :]]
    dot_general x6 -> x0, matrix products: 29.7 us -> none  [the longest x3 19.3 us: block(): lax.dot_general(query, near[0], (((1,), (1,)), ((), ())), preferred_eleme...]
    slice x11 -> x0, local copies, waits for them, and re-layouts: 28.7 us -> none  [the longest x2 11.6 us: body(): own = moved[1:3].reshape(2, FR_DEV, frame_tokens, -1)]
    reduce_sum x4 -> x0, other arithmetic: 19.9 us -> none  [the longest x3 19.7 us: block(): total = jnp.sum(weights.astype(jnp.float32), axis=1, keepdims=True)]
    unnamed x9 -> x1, local copies, waits for them, and re-layouts: 19.9 us -> 2.21 us
    ppermute x2 -> x0, waiting for transfers between devices: 16.5 us -> none  [the longest x1 9.02 us: with_halo(): lax.ppermute(lax.slice_in_dim(block, 0, width, axis=dim), axis, backward)]
  transfers between devices with their start and end apart: 2 -> 0, of which waited for: 2 -> 0; matrix products, arithmetic and copies ran while one was open for 4% -> 0% of each run, Pallas kernels for 0% -> 0%
where the time goes in v1:
time: 55.9 us; the launch traced here: 55.7 us
  Pallas kernels  53.5 us (96%)
  local copies, waits for them, and re-layouts  2.21 us (4%)
    pallas_call x1, Pallas kernels, body(): pl.pallas_call(functools.partial(kernel, frames), out_shape=jax.ShapeDtyp...  53.5 us
    unnamed x1, local copies, waits for them, and re-layouts  2.21 us

profile of v1, /device:TPU:4, one launch (start us, length us, event | category | flops | bytes accessed | tf_op | source)
XLA Modules:
  0.0 55.7 jit_solution(17920070850783111717)
XLA Ops:
  0.0 53.5 %shard_map.55 = bf16[2,5,16,3072]{3,2,1,0:T(8,128)(2,1)} custom-call(s32[3,24]{1,0:T(4,128)} %bitcast.10, s32[1,32]{1,0:T(1,128)} %bitcast.11, bf16[2,5,16,3072]{3,2,1,0:T(8,128)(2,1)} %bitcast.7, bf16[2,5,16,3072]{3,2,1,0:T(8,128)(2,1)} %bitcast.8, bf16[2,5,16,3072]{3,2,1,0:T(8,128)(2,1)} %bitcast.9), custom_call_target="tpu_custom_call" | custom-call | tf_op jit(solution)/shard_map/pallas_call | solution.py:266
  53.5 2.2 %copy.7 = bf16[160,3072]{1,0:T(8,128)(2,1)} copy(bf16[160,3072]{1,0:T(8,128)(2,1)} %bitcast.6) | data formatting | bytes 1966080

commit v2 on v1

--- a/solution.py
+++ b/solution.py
@@ -14,7 +14,7 @@
 PIX = 16
 TW = 10
 LOCAL = 3
-VMEM = 64 * 2**20
+VMEM = 62 * 2**20
 MESH = pl.DeviceIdType.MESH
 BIG = float(2**20)
 SCALE = math.log2(math.e) / math.sqrt(DH)
@@ -94,25 +94,25 @@
 
     order = (5, 1, 4, 3, 6, 2, 7)
 
-    def send_head(head):
-        for at, ref in ((1, k_ref), (2, v_ref), (0, q_ref)):
-            land = qbuf.at[head, me] if at == 0 else kvbuf.at[at - 1, 1, head, me]
-            for step in order:
-                target = peer(step)
-                pltpu.make_async_remote_copy(
-                    src_ref=ref.at[:, :, :, cols(swap(target, frame), head)],
-                    dst_ref=land,
-                    send_sem=send_sem.at[at],
-                    recv_sem=in_sem.at[at, head],
-                    device_id={"frame": frame, "head": target},
-                    device_id_type=MESH,
-                ).start()
-            pltpu.make_async_copy(
-                ref.at[:, :, :, cols(group, head)], land, in_sem.at[at, head]
+    def send(at, head):
+        ref = (q_ref, k_ref, v_ref)[at]
+        land = qbuf.at[head, me] if at == 0 else kvbuf.at[at - 1, 1, head, me]
+        for step in order:
+            target = peer(step)
+            pltpu.make_async_remote_copy(
+                src_ref=ref.at[:, :, :, cols(swap(target, frame), head)],
+                dst_ref=land,
+                send_sem=send_sem.at[at],
+                recv_sem=in_sem.at[at, head],
+                device_id={"frame": frame, "head": target},
+                device_id_type=MESH,
             ).start()
-
-    for head in range(LOCAL):
-        send_head(head)
+        pltpu.make_async_copy(
+            ref.at[:, :, :, cols(group, head)], land, in_sem.at[at, head]
+        ).start()
+
+    for at, head in ((1, 0), (2, 0), (0, 0), (1, 1), (2, 1), (1, 2), (2, 2), (0, 1), (0, 2)):
+        send(at, head)
 
     reach_copy = pltpu.make_async_copy(reach_hbm, reach_ref, small_sem.at[0])
     valid_copy = pltpu.make_async_copy(valid_hbm, valid_ref, small_sem.at[1])
@@ -199,20 +199,19 @@
         result = jnp.where(live_own > 0, result, jnp.float32(0.0)).astype(jnp.bfloat16)
         obuf[head, :, :, pair] = result.reshape(8, ROWS, PIX, DH)
 
-    def send_out(head):
+    def send_out(head, first, last):
+        landing = out_ref.at[:, first:last, :, cols(group, head)]
         for step in order:
             target = peer(step)
             pltpu.make_async_remote_copy(
-                src_ref=obuf.at[head, target],
-                dst_ref=out_ref.at[:, :, :, cols(group, head)],
+                src_ref=obuf.at[head, target, :, first:last],
+                dst_ref=landing,
                 send_sem=out_send_sem,
                 recv_sem=out_sem,
                 device_id={"frame": frame, "head": target},
                 device_id_type=MESH,
             ).start()
-        pltpu.make_async_copy(
-            obuf.at[head, me], out_ref.at[:, :, :, cols(group, head)], out_sem
-        ).start()
+        pltpu.make_async_copy(obuf.at[head, me, :, first:last], landing, out_sem).start()
 
     pass_on(0)
 
@@ -232,9 +231,10 @@
             def _():
                 forward(head, kv, 1).wait_recv()
 
-        for pair in range(PAIRS):
-            attend(head, pair)
-        send_out(head)
+        for first, last in ((0, 3), (3, PAIRS)):
+            for pair in range(first, last):
+                attend(head, pair)
+            send_out(head, first, last)
         return carry
 
     lax.fori_loop(0, LOCAL, per_head, 0)
@@ -265,9 +265,9 @@
         hbm = pl.BlockSpec(memory_space=pltpu.HBM)
         out = pl.pallas_call(
             functools.partial(kernel, frames),
-            out_shape=jax.ShapeDtypeStruct(grid, jnp.bfloat16),
+            out_shape=pltpu.VMEM(grid, jnp.bfloat16),
             in_specs=[hbm] * 5,
-            out_specs=hbm,
+            out_specs=pl.BlockSpec(memory_space=pltpu.VMEM),
             scratch_shapes=[
                 pltpu.VMEM((LOCAL,) + block, jnp.bfloat16),
                 pltpu.VMEM((2, 3, LOCAL) + block, jnp.bfloat16),
@@ -289,9 +289,10 @@
         )(
             head_reach.T,
             frame_valid.reshape(1, frames),
-            queries.reshape(grid),
-            keys.reshape(grid),
-            values.reshape(grid),
+            *(
+                pltpu.with_memory_space_constraint(array.reshape(grid), pltpu.HBM)
+                for array in (queries, keys, values)
+            ),
         )
         return out.reshape(queries.shape)
 

time: 55.9 us -> 53.3 us (0.953)
  Pallas kernels: 53.5 us -> 52.1 us
  local copies, waits for them, and re-layouts: 2.21 us -> 0.95 us
    pallas_call x1, Pallas kernels: 53.5 us -> 52.1 us  [body(): pl.pallas_call(functools.partial(kernel, frames), out_shape=pltpu.VMEM(gr...]
    unnamed x1, local copies, waits for them, and re-layouts: 2.21 us -> 0.95 us
where the time goes in v2:
time: 53.3 us; the launch traced here: 53.1 us
  Pallas kernels  52.1 us (98%)
  local copies, waits for them, and re-layouts  0.95 us (2%)
    pallas_call x1, Pallas kernels, body(): pl.pallas_call(functools.partial(kernel, frames), out_shape=pltpu.VMEM(gr...  52.1 us

profile of v2, /device:TPU:4, one launch (start us, length us, event | category | flops | bytes accessed | tf_op | source)
XLA Modules:
  0.0 53.1 jit_solution(16158756161930826898)
XLA Ops:
  0.0 52.1 %shard_map.55 = bf16[2,5,16,3072]{3,2,1,0:T(8,128)(2,1)S(1)} custom-call(s32[3,24]{1,0:T(4,128)} %bitcast.10, s32[1,32]{1,0:T(1,128)} %bitcast.11, bf16[2,5,16,3072]{3,2,1,0:T(8,128)(2,1)} %bitcast.7, bf16[2,5,16,3072]{3,2,1,0:T(8,128)(2,1)} %bitcast.8, bf16[2,5,16,3072]{3,2,1,0:T(8,128)(2,1)} %bitcast.9), custom_call_target="tpu_custom_call" | custom-call | tf_op jit(solution)/shard_map/pallas_call | solution.py:266
  52.2 0.9 %copy.7 = bf16[160,3072]{1,0:T(8,128)(2,1)} copy(bf16[160,3072]{1,0:T(8,128)(2,1)S(1)} %bitcast.6) | data formatting | bytes 1966080

commit v3 on v2

--- a/solution.py
+++ b/solution.py
@@ -111,7 +111,7 @@
             ref.at[:, :, :, cols(group, head)], land, in_sem.at[at, head]
         ).start()
 
-    for at, head in ((1, 0), (2, 0), (0, 0), (1, 1), (2, 1), (1, 2), (2, 2), (0, 1), (0, 2)):
+    for at, head in ((1, 0), (2, 0), (0, 0), (1, 1), (2, 1), (0, 1), (1, 2), (2, 2), (0, 2)):
         send(at, head)
 
     reach_copy = pltpu.make_async_copy(reach_hbm, reach_ref, small_sem.at[0])
@@ -213,14 +213,16 @@
             ).start()
         pltpu.make_async_copy(obuf.at[head, me, :, first:last], landing, out_sem).start()
 
-    pass_on(0)
-
     def per_head(head, carry):
-        @pl.when(head < LOCAL - 1)
+        pass_on(head)
+        wait_bytes(qbuf.at[head], in_sem.at[0, head])
+        last_head = head == LOCAL - 1
+
+        @pl.when(last_head)
         def _():
-            pass_on(head + 1)
-
-        wait_bytes(qbuf.at[head], in_sem.at[0, head])
+            for done in range(LOCAL - 1):
+                send_out(done, 0, PAIRS)
+
         for kv in range(2):
 
             @pl.when(has_next)
@@ -231,10 +233,14 @@
             def _():
                 forward(head, kv, 1).wait_recv()
 
-        for first, last in ((0, 3), (3, PAIRS)):
+        for first, last in ((0, 2), (2, 4), (4, PAIRS)):
             for pair in range(first, last):
                 attend(head, pair)
-            send_out(head, first, last)
+
+            @pl.when(last_head)
+            def _():
+                send_out(head, first, last)
+
         return carry
 
     lax.fori_loop(0, LOCAL, per_head, 0)

time: 53.3 us -> 66.6 us (1.25)
  Pallas kernels: 52.1 us -> 65.5 us
    pallas_call x1, Pallas kernels: 52.1 us -> 65.5 us  [body(): pl.pallas_call(functools.partial(kernel, frames), out_shape=pltpu.VMEM(gr...]
where the time goes in v3:
time: 66.6 us; the launch traced here: 66.5 us
  Pallas kernels  65.5 us (98%)
  local copies, waits for them, and re-layouts  0.95 us (1%)
    pallas_call x1, Pallas kernels, body(): pl.pallas_call(functools.partial(kernel, frames), out_shape=pltpu.VMEM(gr...  65.5 us

profile of v3, /device:TPU:4, one launch (start us, length us, event | category | flops | bytes accessed | tf_op | source)
XLA Modules:
  0.0 66.5 jit_solution(16383590880113247666)
XLA Ops:
  0.0 65.5 %shard_map.55 = bf16[2,5,16,3072]{3,2,1,0:T(8,128)(2,1)S(1)} custom-call(s32[3,24]{1,0:T(4,128)} %bitcast.10, s32[1,32]{1,0:T(1,128)} %bitcast.11, bf16[2,5,16,3072]{3,2,1,0:T(8,128)(2,1)} %bitcast.7, bf16[2,5,16,3072]{3,2,1,0:T(8,128)(2,1)} %bitcast.8, bf16[2,5,16,3072]{3,2,1,0:T(8,128)(2,1)} %bitcast.9), custom_call_target="tpu_custom_call" | custom-call | tf_op jit(solution)/shard_map/pallas_call | solution.py:272
  65.5 0.9 %copy.7 = bf16[160,3072]{1,0:T(8,128)(2,1)} copy(bf16[160,3072]{1,0:T(8,128)(2,1)S(1)} %bitcast.6) | data formatting | bytes 1966080

commit v4 on v3

--- a/solution.py
+++ b/solution.py
@@ -141,17 +141,16 @@
             device_id_type=MESH,
         )
 
-    def pass_on(head):
-        for kv in range(2):
-            wait_bytes(kvbuf.at[kv, 1, head], in_sem.at[kv + 1, head])
-
-            @pl.when(has_prev)
-            def _():
-                forward(head, kv, 0).start()
-
-            @pl.when(has_next)
-            def _():
-                forward(head, kv, 1).start()
+    def pass_on(head, kv):
+        wait_bytes(kvbuf.at[kv, 1, head], in_sem.at[kv + 1, head])
+
+        @pl.when(has_prev)
+        def _():
+            forward(head, kv, 0).start()
+
+        @pl.when(has_next)
+        def _():
+            forward(head, kv, 1).start()
 
     reach_copy.wait()
     valid_copy.wait()
@@ -213,10 +212,12 @@
             ).start()
         pltpu.make_async_copy(obuf.at[head, me, :, first:last], landing, out_sem).start()
 
+    pass_on(0, 0)
+    pass_on(0, 1)
+
     def per_head(head, carry):
-        pass_on(head)
+        last_head = head == LOCAL - 1
         wait_bytes(qbuf.at[head], in_sem.at[0, head])
-        last_head = head == LOCAL - 1
 
         @pl.when(last_head)
         def _():
@@ -233,13 +234,19 @@
             def _():
                 forward(head, kv, 1).wait_recv()
 
-        for first, last in ((0, 2), (2, 4), (4, PAIRS)):
+        for first, last, kv in ((0, 2, 0), (2, 4, None), (4, PAIRS, 1)):
             for pair in range(first, last):
                 attend(head, pair)
 
             @pl.when(last_head)
             def _():
                 send_out(head, first, last)
+
+            if kv is not None:
+
+                @pl.when(jnp.logical_not(last_head))
+                def _():
+                    pass_on(head + 1, kv)
 
         return carry
 

time: 66.6 us -> 59.9 us (0.90)
  Pallas kernels: 65.5 us -> 58.8 us
    pallas_call x1, Pallas kernels: 65.5 us -> 58.8 us  [body(): pl.pallas_call(functools.partial(kernel, frames), out_shape=pltpu.VMEM(gr...]
where the time goes in v4:
time: 59.9 us; the launch traced here: 59.8 us
  Pallas kernels  58.8 us (98%)
  local copies, waits for them, and re-layouts  0.95 us (2%)
    pallas_call x1, Pallas kernels, body(): pl.pallas_call(functools.partial(kernel, frames), out_shape=pltpu.VMEM(gr...  58.8 us

profile of v4, /device:TPU:4, one launch (start us, length us, event | category | flops | bytes accessed | tf_op | source)
XLA Modules:
  0.0 59.8 jit_solution(5153200434657268032)
XLA Ops:
  0.0 58.8 %shard_map.55 = bf16[2,5,16,3072]{3,2,1,0:T(8,128)(2,1)S(1)} custom-call(s32[3,24]{1,0:T(4,128)} %bitcast.10, s32[1,32]{1,0:T(1,128)} %bitcast.11, bf16[2,5,16,3072]{3,2,1,0:T(8,128)(2,1)} %bitcast.7, bf16[2,5,16,3072]{3,2,1,0:T(8,128)(2,1)} %bitcast.8, bf16[2,5,16,3072]{3,2,1,0:T(8,128)(2,1)} %bitcast.9), custom_call_target="tpu_custom_call" | custom-call | tf_op jit(solution)/shard_map/pallas_call | solution.py:279
  58.8 0.9 %copy.7 = bf16[160,3072]{1,0:T(8,128)(2,1)} copy(bf16[160,3072]{1,0:T(8,128)(2,1)S(1)} %bitcast.6) | data formatting | bytes 1966080

commit v5 on v2

--- a/solution.py
+++ b/solution.py
@@ -14,6 +14,7 @@
 PIX = 16
 TW = 10
 LOCAL = 3
+BLOCK = 8 * ROWS * PIX
 VMEM = 62 * 2**20
 MESH = pl.DeviceIdType.MESH
 BIG = float(2**20)
@@ -21,7 +22,7 @@
 
 
 def query_features(pair, reach_h, reach_w):
-    shape = (8 * ROWS * PIX, DH)
+    shape = (BLOCK, DH)
     row = lax.broadcasted_iota(jnp.int32, shape, 0)
     col = lax.broadcasted_iota(jnp.int32, shape, 1)
     tile_y = row >> 7
@@ -51,7 +52,7 @@
 
 def kernel(
     frames, reach_hbm, valid_hbm, q_ref, k_ref, v_ref, out_ref,
-    qbuf, kvbuf, kfeat, obuf, reach_ref, valid_ref,
+    qbuf, kvbuf, kfeat, vturn, obuf, reach_ref, valid_ref,
     send_sem, in_sem, fwd_sem, halo_sem, out_send_sem, out_sem, small_sem,
 ):
     frame = lax.axis_index("frame")
@@ -123,6 +124,8 @@
         for pair in range(PAIRS):
             kfeat[part, :, pair] = key_features(part, pair)
 
+    vturn[:, DH:] = jnp.ones((3, 16, PAIRS * BLOCK), jnp.bfloat16)
+
     @pl.when(jnp.logical_not(has_prev))
     def _():
         kvbuf[:, 0] = jnp.zeros(kvbuf.shape[:1] + kvbuf.shape[2:], jnp.bfloat16)
@@ -159,44 +162,46 @@
     live_prev = jnp.where(has_prev, valid_ref[0, jnp.maximum(frame - 1, 0)], 0)
     live_next = jnp.where(has_next, valid_ref[0, jnp.minimum(frame + 1, frames - 1)], 0)
 
+    def turn_values(head):
+        for slot in range(3):
+            for pair in range(PAIRS):
+                values = kvbuf[1, slot, head, :, :, pair].reshape(BLOCK, DH)
+                vturn[slot, :DH, pair * BLOCK : (pair + 1) * BLOCK] = values.T
+
     def attend(head, pair):
         row = group * LOCAL + head
-        reach_t = reach_ref[0, row]
         base = query_features(pair, reach_ref[1, row], reach_ref[2, row])
-        near = reach_t >= 1
+        near = reach_ref[0, row] >= 1
         allowed = ((live_prev > 0) & near, live_own > 0, (live_next > 0) & near)
-        query = qbuf[head, :, :, pair].reshape(8 * ROWS * PIX, DH)
+        query = qbuf[head, :, :, pair].reshape(BLOCK, DH)
         first, last = max(pair - 1, 0), min(pair + 2, PAIRS)
-        count = 8 * ROWS * (last - first) * PIX
-        tiles = kfeat[:, :, first:last].reshape(count, DH)
         scores = []
         for slot in range(3):
             features = jnp.minimum(
                 base, jnp.where(allowed[slot], jnp.float32(0.0), jnp.float32(-BIG))
             ).astype(jnp.bfloat16)
-            keys = kvbuf[0, slot, head, :, :, first:last].reshape(count, DH)
-            scores.append(
-                lax.dot_general(
-                    jnp.concatenate([query, features], axis=1),
-                    jnp.concatenate([keys, tiles], axis=1),
-                    (((1,), (1,)), ((), ())),
-                    preferred_element_type=jnp.float32,
+            stationary = jnp.concatenate([query, features], axis=1)
+            for at in range(first, last):
+                keys = kvbuf[0, slot, head, :, :, at].reshape(BLOCK, DH)
+                tiles = kfeat[:, :, at].reshape(BLOCK, DH)
+                scores.append(
+                    lax.dot_general(
+                        jnp.concatenate([keys, tiles], axis=1),
+                        stationary,
+                        (((1,), (1,)), ((), ())),
+                        preferred_element_type=jnp.float32,
+                    )
                 )
-            )
-        top = functools.reduce(jnp.maximum, [jnp.max(s, axis=1, keepdims=True) for s in scores])
-        ones = jnp.ones((count, DH), jnp.bfloat16)
-        mixed = None
-        for slot in range(3):
-            weights = jnp.exp2((scores[slot] - top) * SCALE).astype(jnp.bfloat16)
-            values = kvbuf[1, slot, head, :, :, first:last].reshape(count, DH)
-            term = jnp.dot(
-                weights,
-                jnp.concatenate([values, ones], axis=1),
-                preferred_element_type=jnp.float32,
-            )
-            mixed = term if mixed is None else mixed + term
-        result = mixed[:, :DH] / mixed[:, DH:]
-        result = jnp.where(live_own > 0, result, jnp.float32(0.0)).astype(jnp.bfloat16)
+        top = jnp.max(functools.reduce(jnp.maximum, scores), axis=0, keepdims=True)
+        weights = jnp.concatenate(
+            [jnp.exp2((s - top) * SCALE).astype(jnp.bfloat16) for s in scores], axis=0
+        )
+        turned = jnp.concatenate(
+            [vturn[slot, :, first * BLOCK : last * BLOCK] for slot in range(3)], axis=1
+        )
+        mixed = jnp.dot(turned, weights, preferred_element_type=jnp.float32)
+        result = mixed[:DH] / mixed[DH : DH + 1]
+        result = jnp.where(live_own > 0, result, jnp.float32(0.0)).T.astype(jnp.bfloat16)
         obuf[head, :, :, pair] = result.reshape(8, ROWS, PIX, DH)
 
     def send_out(head, first, last):
@@ -231,6 +236,7 @@
             def _():
                 forward(head, kv, 1).wait_recv()
 
+        turn_values(head)
         for first, last in ((0, 3), (3, PAIRS)):
             for pair in range(first, last):
                 attend(head, pair)
@@ -272,6 +278,7 @@
                 pltpu.VMEM((LOCAL,) + block, jnp.bfloat16),
                 pltpu.VMEM((2, 3, LOCAL) + block, jnp.bfloat16),
                 pltpu.VMEM(block, jnp.bfloat16),
+                pltpu.VMEM((3, DH + 16, PAIRS * BLOCK), jnp.bfloat16),
                 pltpu.VMEM((LOCAL,) + block, jnp.bfloat16),
                 pltpu.SMEM((3, head_reach.shape[0]), jnp.int32),
                 pltpu.SMEM((1, frames), jnp.int32),

time: 53.3 us -> 54.3 us (1.019)
  Pallas kernels: 52.1 us -> 53.1 us
    pallas_call x1, Pallas kernels: 52.1 us -> 53.1 us  [body(): pl.pallas_call(functools.partial(kernel, frames), out_shape=pltpu.VMEM(gr...]
where the time goes in v5:
time: 54.3 us; the launch traced here: 54 us
  Pallas kernels  53.1 us (98%)
  local copies, waits for them, and re-layouts  0.95 us (2%)
    pallas_call x1, Pallas kernels, body(): pl.pallas_call(functools.partial(kernel, frames), out_shape=pltpu.VMEM(gr...  53.1 us

profile of v5, /device:TPU:4, one launch (start us, length us, event | category | flops | bytes accessed | tf_op | source)
XLA Modules:
  0.0 54.0 jit_solution(16872180904051716577)
XLA Ops:
  0.0 53.1 %shard_map.55 = bf16[2,5,16,3072]{3,2,1,0:T(8,128)(2,1)S(1)} custom-call(s32[3,24]{1,0:T(4,128)} %bitcast.10, s32[1,32]{1,0:T(1,128)} %bitcast.11, bf16[2,5,16,3072]{3,2,1,0:T(8,128)(2,1)} %bitcast.7, bf16[2,5,16,3072]{3,2,1,0:T(8,128)(2,1)} %bitcast.8, bf16[2,5,16,3072]{3,2,1,0:T(8,128)(2,1)} %bitcast.9), custom_call_target="tpu_custom_call" | custom-call | tf_op jit(solution)/shard_map/pallas_call | solution.py:272
  53.1 0.9 %copy.7 = bf16[160,3072]{1,0:T(8,128)(2,1)} copy(bf16[160,3072]{1,0:T(8,128)(2,1)S(1)} %bitcast.6) | data formatting | bytes 1966080

commit v6 on v5

--- a/solution.py
+++ b/solution.py
@@ -22,9 +22,9 @@
 
 
 def query_features(pair, reach_h, reach_w):
-    shape = (BLOCK, DH)
-    row = lax.broadcasted_iota(jnp.int32, shape, 0)
-    col = lax.broadcasted_iota(jnp.int32, shape, 1)
+    shape = (DH, BLOCK)
+    row = lax.broadcasted_iota(jnp.int32, shape, 1)
+    col = lax.broadcasted_iota(jnp.int32, shape, 0)
     tile_y = row >> 7
     tile_x = 2 * pair + ((row & 15) >> 3)
     key_y = (col >= TW).astype(jnp.int32)
@@ -52,7 +52,7 @@
 
 def kernel(
     frames, reach_hbm, valid_hbm, q_ref, k_ref, v_ref, out_ref,
-    qbuf, kvbuf, kfeat, vturn, obuf, reach_ref, valid_ref,
+    qbuf, kvbuf, kfeat, qfeat, vturn, obuf, reach_ref, valid_ref,
     send_sem, in_sem, fwd_sem, halo_sem, out_send_sem, out_sem, small_sem,
 ):
     frame = lax.axis_index("frame")
@@ -162,6 +162,19 @@
     live_prev = jnp.where(has_prev, valid_ref[0, jnp.maximum(frame - 1, 0)], 0)
     live_next = jnp.where(has_next, valid_ref[0, jnp.minimum(frame + 1, frames - 1)], 0)
 
+    def mask_rows(head, carry):
+        row = group * LOCAL + head
+        near = reach_ref[0, row] >= 1
+        allowed = ((live_prev > 0) & near, live_own > 0, (live_next > 0) & near)
+        for pair in range(PAIRS):
+            base = query_features(pair, reach_ref[1, row], reach_ref[2, row])
+            for slot in range(3):
+                level = jnp.where(allowed[slot], jnp.float32(0.0), jnp.float32(-BIG))
+                qfeat[head, pair, slot] = jnp.minimum(base, level).astype(jnp.bfloat16)
+        return carry
+
+    lax.fori_loop(0, LOCAL, mask_rows, 0)
+
     def turn_values(head):
         for slot in range(3):
             for pair in range(PAIRS):
@@ -169,26 +182,18 @@
                 vturn[slot, :DH, pair * BLOCK : (pair + 1) * BLOCK] = values.T
 
     def attend(head, pair):
-        row = group * LOCAL + head
-        base = query_features(pair, reach_ref[1, row], reach_ref[2, row])
-        near = reach_ref[0, row] >= 1
-        allowed = ((live_prev > 0) & near, live_own > 0, (live_next > 0) & near)
-        query = qbuf[head, :, :, pair].reshape(BLOCK, DH)
+        query = qbuf[head, :, :, pair].reshape(BLOCK, DH).T
         first, last = max(pair - 1, 0), min(pair + 2, PAIRS)
         scores = []
         for slot in range(3):
-            features = jnp.minimum(
-                base, jnp.where(allowed[slot], jnp.float32(0.0), jnp.float32(-BIG))
-            ).astype(jnp.bfloat16)
-            stationary = jnp.concatenate([query, features], axis=1)
+            stationary = jnp.concatenate([query, qfeat[head, pair, slot]], axis=0)
             for at in range(first, last):
                 keys = kvbuf[0, slot, head, :, :, at].reshape(BLOCK, DH)
                 tiles = kfeat[:, :, at].reshape(BLOCK, DH)
                 scores.append(
-                    lax.dot_general(
+                    jnp.dot(
                         jnp.concatenate([keys, tiles], axis=1),
                         stationary,
-                        (((1,), (1,)), ((), ())),
                         preferred_element_type=jnp.float32,
                     )
                 )
@@ -278,6 +283,7 @@
                 pltpu.VMEM((LOCAL,) + block, jnp.bfloat16),
                 pltpu.VMEM((2, 3, LOCAL) + block, jnp.bfloat16),
                 pltpu.VMEM(block, jnp.bfloat16),
+                pltpu.VMEM((LOCAL, PAIRS, 3, DH, BLOCK), jnp.bfloat16),
                 pltpu.VMEM((3, DH + 16, PAIRS * BLOCK), jnp.bfloat16),
                 pltpu.VMEM((LOCAL,) + block, jnp.bfloat16),
                 pltpu.SMEM((3, head_reach.shape[0]), jnp.int32),

time: 54.3 us -> 54.5 us (level)
  no operation moved by 1% of the time
where the time goes in v6:
time: 54.5 us; the launch traced here: 54.3 us
  Pallas kernels  53.3 us (98%)
  local copies, waits for them, and re-layouts  0.95 us (2%)
    pallas_call x1, Pallas kernels, body(): pl.pallas_call(functools.partial(kernel, frames), out_shape=pltpu.VMEM(gr...  53.3 us

profile of v6, /device:TPU:4, one launch (start us, length us, event | category | flops | bytes accessed | tf_op | source)
XLA Modules:
  0.0 54.3 jit_solution(12849187096994848264)
XLA Ops:
  0.0 53.3 %shard_map.55 = bf16[2,5,16,3072]{3,2,1,0:T(8,128)(2,1)S(1)} custom-call(s32[3,24]{1,0:T(4,128)} %bitcast.10, s32[1,32]{1,0:T(1,128)} %bitcast.11, bf16[2,5,16,3072]{3,2,1,0:T(8,128)(2,1)} %bitcast.7, bf16[2,5,16,3072]{3,2,1,0:T(8,128)(2,1)} %bitcast.8, bf16[2,5,16,3072]{3,2,1,0:T(8,128)(2,1)} %bitcast.9), custom_call_target="tpu_custom_call" | custom-call | tf_op jit(solution)/shard_map/pallas_call | solution.py:277
  53.3 0.9 %copy.7 = bf16[160,3072]{1,0:T(8,128)(2,1)} copy(bf16[160,3072]{1,0:T(8,128)(2,1)S(1)} %bitcast.6) | data formatting | bytes 1966080

commit v7 on v2

--- a/solution.py
+++ b/solution.py
@@ -62,10 +62,19 @@
         return lax.rem(index + jnp.where(at >= half, 4, 0), 8)
 
     group = swap(me, frame)
-    has_prev = frame > 0
-    has_next = frame < frames - 1
-    prev_id = {"frame": frame - 1, "head": swap(group, frame - 1)}
-    next_id = {"frame": frame + 1, "head": swap(group, frame + 1)}
+    odd = lax.rem(frame, 2)
+    way = 2 * odd - 1
+    z_slot, mate_slot = 2 * odd, 2 - 2 * odd
+    has_z = (frame + way >= 0) & (frame + way < frames)
+    has_relay = (frame - 2 * way >= 0) & (frame - 2 * way < frames)
+
+    def device(at):
+        return {"frame": at, "head": swap(group, at)}
+
+    mate_id = device(frame - way)
+    z_id = device(frame + way)
+    z_far_id = device(frame + 2 * way)
+    relay_id = device(frame - 2 * way)
 
     def peer(step):
         part = lax.rem(me // 4 + step // 4, 2) * 4 + lax.rem(me + step, 4)
@@ -77,16 +86,19 @@
             barrier, inc=1, device_id={"frame": frame, "head": peer(step)}, device_id_type=MESH
         )
 
-    @pl.when(has_prev)
+    pl.semaphore_signal(barrier, inc=1, device_id=mate_id, device_id_type=MESH)
+
+    @pl.when(has_z)
     def _():
-        pl.semaphore_signal(barrier, inc=1, device_id=prev_id, device_id_type=MESH)
-
-    @pl.when(has_next)
+        pl.semaphore_signal(barrier, inc=1, device_id=z_id, device_id_type=MESH)
+        pl.semaphore_signal(barrier, inc=1, device_id=z_far_id, device_id_type=MESH)
+
+    @pl.when(has_relay)
     def _():
-        pl.semaphore_signal(barrier, inc=1, device_id=next_id, device_id_type=MESH)
+        pl.semaphore_signal(barrier, inc=1, device_id=relay_id, device_id_type=MESH)
 
     pl.semaphore_wait(
-        barrier, 7 + jnp.where(has_prev, 1, 0) + jnp.where(has_next, 1, 0)
+        barrier, 8 + jnp.where(has_z, 2, 0) + jnp.where(has_relay, 1, 0)
     )
 
     def cols(of_group, head):
@@ -123,41 +135,52 @@
         for pair in range(PAIRS):
             kfeat[part, :, pair] = key_features(part, pair)
 
-    @pl.when(jnp.logical_not(has_prev))
+    @pl.when(jnp.logical_not(has_z))
     def _():
-        kvbuf[:, 0] = jnp.zeros(kvbuf.shape[:1] + kvbuf.shape[2:], jnp.bfloat16)
-
-    @pl.when(jnp.logical_not(has_next))
-    def _():
-        kvbuf[:, 2] = jnp.zeros(kvbuf.shape[:1] + kvbuf.shape[2:], jnp.bfloat16)
-
-    def forward(head, kv, way):
+        kvbuf[:, z_slot] = jnp.zeros(kvbuf.shape[:1] + kvbuf.shape[2:], jnp.bfloat16)
+
+    def forward(head, kv, side, from_slot, to_slot, target):
         return pltpu.make_async_remote_copy(
-            src_ref=kvbuf.at[kv, 1, head],
-            dst_ref=kvbuf.at[kv, 2 - 2 * way, head],
-            send_sem=fwd_sem.at[kv, way, head],
-            recv_sem=halo_sem.at[kv, way, head],
-            device_id=(prev_id, next_id)[way],
+            src_ref=kvbuf.at[kv, from_slot, head],
+            dst_ref=kvbuf.at[kv, to_slot, head],
+            send_sem=fwd_sem.at[kv, side, head],
+            recv_sem=halo_sem.at[kv, side, head],
+            device_id=target,
             device_id_type=MESH,
         )
 
+    def to_mate(head, kv):
+        return forward(head, kv, 0, 1, z_slot, mate_id)
+
+    def values_to_z(head):
+        return forward(head, 1, 1, 1, mate_slot, z_id)
+
+    def relay_keys(head):
+        return forward(head, 0, 1, mate_slot, z_slot, relay_id)
+
     def pass_on(head):
-        for kv in range(2):
-            wait_bytes(kvbuf.at[kv, 1, head], in_sem.at[kv + 1, head])
-
-            @pl.when(has_prev)
-            def _():
-                forward(head, kv, 0).start()
-
-            @pl.when(has_next)
-            def _():
-                forward(head, kv, 1).start()
+        wait_bytes(kvbuf.at[0, 1, head], in_sem.at[1, head])
+        to_mate(head, 0).start()
+        wait_bytes(kvbuf.at[1, 1, head], in_sem.at[2, head])
+
+        @pl.when(has_z)
+        def _():
+            values_to_z(head).start()
+
+        to_mate(head, 1).start()
+        to_mate(head, 0).wait_recv()
+
+        @pl.when(has_relay)
+        def _():
+            relay_keys(head).start()
 
     reach_copy.wait()
     valid_copy.wait()
     live_own = valid_ref[0, frame]
-    live_prev = jnp.where(has_prev, valid_ref[0, jnp.maximum(frame - 1, 0)], 0)
-    live_next = jnp.where(has_next, valid_ref[0, jnp.minimum(frame + 1, frames - 1)], 0)
+    live_prev = jnp.where(frame > 0, valid_ref[0, jnp.maximum(frame - 1, 0)], 0)
+    live_next = jnp.where(
+        frame < frames - 1, valid_ref[0, jnp.minimum(frame + 1, frames - 1)], 0
+    )
 
     def attend(head, pair):
         row = group * LOCAL + head
@@ -221,15 +244,12 @@
             pass_on(head + 1)
 
         wait_bytes(qbuf.at[head], in_sem.at[0, head])
-        for kv in range(2):
-
-            @pl.when(has_next)
-            def _():
-                forward(head, kv, 0).wait_recv()
-
-            @pl.when(has_prev)
-            def _():
-                forward(head, kv, 1).wait_recv()
+        to_mate(head, 1).wait_recv()
+
+        @pl.when(has_z)
+        def _():
+            relay_keys(head).wait_recv()
+            values_to_z(head).wait_recv()
 
         for first, last in ((0, 3), (3, PAIRS)):
             for pair in range(first, last):
@@ -242,15 +262,16 @@
     for at in range(3):
         wait_bytes(qbuf.at[:, 0:7], send_sem.at[at])
     for head in range(LOCAL):
-        for kv in range(2):
-
-            @pl.when(has_prev)
-            def _():
-                forward(head, kv, 0).wait_send()
-
-            @pl.when(has_next)
-            def _():
-                forward(head, kv, 1).wait_send()
+        to_mate(head, 0).wait_send()
+        to_mate(head, 1).wait_send()
+
+        @pl.when(has_z)
+        def _():
+            values_to_z(head).wait_send()
+
+        @pl.when(has_relay)
+        def _():
+            relay_keys(head).wait_send()
 
     wait_bytes(obuf.at[:, 0:7], out_send_sem)
     wait_bytes(obuf, out_sem)

time: 53.3 us -> 54.6 us (1.024)
  Pallas kernels: 52.1 us -> 53.5 us
    pallas_call x1, Pallas kernels: 52.1 us -> 53.5 us  [body(): pl.pallas_call(functools.partial(kernel, frames), out_shape=pltpu.VMEM(gr...]
where the time goes in v7:
time: 54.6 us; the launch traced here: 54.5 us
  Pallas kernels  53.5 us (98%)
  local copies, waits for them, and re-layouts  0.95 us (2%)
    pallas_call x1, Pallas kernels, body(): pl.pallas_call(functools.partial(kernel, frames), out_shape=pltpu.VMEM(gr...  53.5 us

profile of v7, /device:TPU:4, one launch (start us, length us, event | category | flops | bytes accessed | tf_op | source)
XLA Modules:
  0.0 54.5 jit_solution(6412193721766715752)
XLA Ops:
  0.0 53.5 %shard_map.55 = bf16[2,5,16,3072]{3,2,1,0:T(8,128)(2,1)S(1)} custom-call(s32[3,24]{1,0:T(4,128)} %bitcast.10, s32[1,32]{1,0:T(1,128)} %bitcast.11, bf16[2,5,16,3072]{3,2,1,0:T(8,128)(2,1)} %bitcast.7, bf16[2,5,16,3072]{3,2,1,0:T(8,128)(2,1)} %bitcast.8, bf16[2,5,16,3072]{3,2,1,0:T(8,128)(2,1)} %bitcast.9), custom_call_target="tpu_custom_call" | custom-call | tf_op jit(solution)/shard_map/pallas_call | solution.py:287
  53.5 0.9 %copy.7 = bf16[160,3072]{1,0:T(8,128)(2,1)} copy(bf16[160,3072]{1,0:T(8,128)(2,1)S(1)} %bitcast.6) | data formatting | bytes 1966080

commit v8 on v7

--- a/solution.py
+++ b/solution.py
@@ -52,7 +52,7 @@
 def kernel(
     frames, reach_hbm, valid_hbm, q_ref, k_ref, v_ref, out_ref,
     qbuf, kvbuf, kfeat, obuf, reach_ref, valid_ref,
-    send_sem, in_sem, fwd_sem, halo_sem, out_send_sem, out_sem, small_sem,
+    send_sem, in_sem, fwd_sem, halo_sem, out_send_sem, out_sem, small_sem, ready_sem,
 ):
     frame = lax.axis_index("frame")
     me = lax.axis_index("head")
@@ -88,18 +88,24 @@
 
     pl.semaphore_signal(barrier, inc=1, device_id=mate_id, device_id_type=MESH)
 
-    @pl.when(has_z)
+    even = odd == 0
+
+    @pl.when(even & has_z)
     def _():
         pl.semaphore_signal(barrier, inc=1, device_id=z_id, device_id_type=MESH)
         pl.semaphore_signal(barrier, inc=1, device_id=z_far_id, device_id_type=MESH)
 
-    @pl.when(has_relay)
+    @pl.when((odd == 1) & has_relay)
     def _():
         pl.semaphore_signal(barrier, inc=1, device_id=relay_id, device_id_type=MESH)
 
-    pl.semaphore_wait(
-        barrier, 8 + jnp.where(has_z, 2, 0) + jnp.where(has_relay, 1, 0)
-    )
+    greeted = jnp.where(even, jnp.where(has_relay, 1, 0), jnp.where(has_z, 2, 0))
+    pl.semaphore_wait(barrier, 8 + greeted)
+
+    @pl.when((odd == 1) & has_z)
+    def _():
+        pl.semaphore_signal(ready_sem, inc=1, device_id=z_id, device_id_type=MESH)
+        pl.semaphore_signal(ready_sem, inc=1, device_id=z_far_id, device_id_type=MESH)
 
     def cols(of_group, head):
         return pl.ds(pl.multiple_of((of_group * LOCAL + head) * DH, DH), DH)
@@ -236,6 +242,10 @@
             ).start()
         pltpu.make_async_copy(obuf.at[head, me, :, first:last], landing, out_sem).start()
 
+    @pl.when(jnp.where(even, has_z, has_relay))
+    def _():
+        pl.semaphore_wait(ready_sem, 1)
+
     pass_on(0)
 
     def per_head(head, carry):
@@ -244,6 +254,13 @@
             pass_on(head + 1)
 
         wait_bytes(qbuf.at[head], in_sem.at[0, head])
+        last_head = head == LOCAL - 1
+
+        @pl.when(last_head)
+        def _():
+            for done in range(LOCAL - 1):
+                send_out(done, 0, PAIRS)
+
         to_mate(head, 1).wait_recv()
 
         @pl.when(has_z)
@@ -251,10 +268,14 @@
             relay_keys(head).wait_recv()
             values_to_z(head).wait_recv()
 
-        for first, last in ((0, 3), (3, PAIRS)):
+        for first, last in ((0, 2), (2, 4), (4, PAIRS)):
             for pair in range(first, last):
                 attend(head, pair)
-            send_out(head, first, last)
+
+            @pl.when(last_head)
+            def _():
+                send_out(head, first, last)
+
         return carry
 
     lax.fori_loop(0, LOCAL, per_head, 0)
@@ -303,6 +324,7 @@
                 pltpu.SemaphoreType.DMA,
                 pltpu.SemaphoreType.DMA,
                 pltpu.SemaphoreType.DMA((2,)),
+                pltpu.SemaphoreType.REGULAR,
             ],
             compiler_params=pltpu.CompilerParams(
                 collective_id=0, has_side_effects=True, vmem_limit_bytes=VMEM

time: 54.6 us -> 55.6 us (1.018)
  Pallas kernels: 53.5 us -> 54.3 us
    pallas_call x1, Pallas kernels: 53.5 us -> 54.3 us  [body(): pl.pallas_call(functools.partial(kernel, frames), out_shape=pltpu.VMEM(gr...]
where the time goes in v8:
time: 55.6 us; the launch traced here: 55.2 us
  Pallas kernels  54.3 us (98%)
  local copies, waits for them, and re-layouts  0.95 us (2%)
    pallas_call x1, Pallas kernels, body(): pl.pallas_call(functools.partial(kernel, frames), out_shape=pltpu.VMEM(gr...  54.3 us

profile of v8, /device:TPU:4, one launch (start us, length us, event | category | flops | bytes accessed | tf_op | source)
XLA Modules:
  0.0 55.2 jit_solution(5873534196745764543)
XLA Ops:
  0.0 54.3 %shard_map.55 = bf16[2,5,16,3072]{3,2,1,0:T(8,128)(2,1)S(1)} custom-call(s32[3,24]{1,0:T(4,128)} %bitcast.10, s32[1,32]{1,0:T(1,128)} %bitcast.11, bf16[2,5,16,3072]{3,2,1,0:T(8,128)(2,1)} %bitcast.7, bf16[2,5,16,3072]{3,2,1,0:T(8,128)(2,1)} %bitcast.8, bf16[2,5,16,3072]{3,2,1,0:T(8,128)(2,1)} %bitcast.9), custom_call_target="tpu_custom_call" | custom-call | tf_op jit(solution)/shard_map/pallas_call | solution.py:308
  54.3 0.9 %copy.7 = bf16[160,3072]{1,0:T(8,128)(2,1)} copy(bf16[160,3072]{1,0:T(8,128)(2,1)S(1)} %bitcast.6) | data formatting | bytes 1966080

commit v9 on v2

--- a/solution.py
+++ b/solution.py
@@ -52,7 +52,7 @@
 def kernel(
     frames, reach_hbm, valid_hbm, q_ref, k_ref, v_ref, out_ref,
     qbuf, kvbuf, kfeat, obuf, reach_ref, valid_ref,
-    send_sem, in_sem, fwd_sem, halo_sem, out_send_sem, out_sem, small_sem,
+    send_sem, in_sem, fwd_sem, halo_sem, out_send_sem, out_sem, small_sem, ready_sem,
 ):
     frame = lax.axis_index("frame")
     me = lax.axis_index("head")
@@ -77,17 +77,25 @@
             barrier, inc=1, device_id={"frame": frame, "head": peer(step)}, device_id_type=MESH
         )
 
+    even = lax.rem(frame, 2) == 0
+    odd = jnp.logical_not(even)
+
+    def greet(sem, target):
+        pl.semaphore_signal(sem, inc=1, device_id=target, device_id_type=MESH)
+
     @pl.when(has_prev)
     def _():
-        pl.semaphore_signal(barrier, inc=1, device_id=prev_id, device_id_type=MESH)
-
-    @pl.when(has_next)
-    def _():
-        pl.semaphore_signal(barrier, inc=1, device_id=next_id, device_id_type=MESH)
-
-    pl.semaphore_wait(
-        barrier, 7 + jnp.where(has_prev, 1, 0) + jnp.where(has_next, 1, 0)
-    )
+        greet(barrier, prev_id)
+
+    @pl.when(even)
+    def _():
+        greet(barrier, next_id)
+
+    pl.semaphore_wait(barrier, 8 + jnp.where(odd & has_next, 1, 0))
+
+    @pl.when(odd & has_next)
+    def _():
+        greet(ready_sem, next_id)
 
     def cols(of_group, head):
         return pl.ds(pl.multiple_of((of_group * LOCAL + head) * DH, DH), DH)
@@ -166,15 +174,15 @@
         near = reach_t >= 1
         allowed = ((live_prev > 0) & near, live_own > 0, (live_next > 0) & near)
         query = qbuf[head, :, :, pair].reshape(8 * ROWS * PIX, DH)
-        first, last = max(pair - 1, 0), min(pair + 2, PAIRS)
-        count = 8 * ROWS * (last - first) * PIX
-        tiles = kfeat[:, :, first:last].reshape(count, DH)
+        near_pairs = pl.ds(jnp.clip(pair - 1, 0, PAIRS - 3), 3)
+        count = 8 * ROWS * 3 * PIX
+        tiles = kfeat[:, :, near_pairs].reshape(count, DH)
         scores = []
         for slot in range(3):
             features = jnp.minimum(
                 base, jnp.where(allowed[slot], jnp.float32(0.0), jnp.float32(-BIG))
             ).astype(jnp.bfloat16)
-            keys = kvbuf[0, slot, head, :, :, first:last].reshape(count, DH)
+            keys = kvbuf[0, slot, head, :, :, near_pairs].reshape(count, DH)
             scores.append(
                 lax.dot_general(
                     jnp.concatenate([query, features], axis=1),
@@ -183,12 +191,12 @@
                     preferred_element_type=jnp.float32,
                 )
             )
-        top = functools.reduce(jnp.maximum, [jnp.max(s, axis=1, keepdims=True) for s in scores])
+        top = jnp.max(functools.reduce(jnp.maximum, scores), axis=1, keepdims=True)
         ones = jnp.ones((count, DH), jnp.bfloat16)
         mixed = None
         for slot in range(3):
             weights = jnp.exp2((scores[slot] - top) * SCALE).astype(jnp.bfloat16)
-            values = kvbuf[1, slot, head, :, :, first:last].reshape(count, DH)
+            values = kvbuf[1, slot, head, :, :, near_pairs].reshape(count, DH)
             term = jnp.dot(
                 weights,
                 jnp.concatenate([values, ones], axis=1),
@@ -213,6 +221,10 @@
             ).start()
         pltpu.make_async_copy(obuf.at[head, me, :, first:last], landing, out_sem).start()
 
+    @pl.when(even & has_prev)
+    def _():
+        pl.semaphore_wait(ready_sem, 1)
+
     pass_on(0)
 
     def per_head(head, carry):
@@ -231,10 +243,17 @@
             def _():
                 forward(head, kv, 1).wait_recv()
 
-        for first, last in ((0, 3), (3, PAIRS)):
-            for pair in range(first, last):
-                attend(head, pair)
-            send_out(head, first, last)
+        def per_pair(pair, carry):
+            attend(head, pair)
+            for first, last in ((0, 3), (3, PAIRS)):
+
+                @pl.when(pair == last - 1)
+                def _():
+                    send_out(head, first, last)
+
+            return carry
+
+        lax.fori_loop(0, PAIRS, per_pair, 0)
         return carry
 
     lax.fori_loop(0, LOCAL, per_head, 0)
@@ -282,6 +301,7 @@
                 pltpu.SemaphoreType.DMA,
                 pltpu.SemaphoreType.DMA,
                 pltpu.SemaphoreType.DMA((2,)),
+                pltpu.SemaphoreType.REGULAR,
             ],
             compiler_params=pltpu.CompilerParams(
                 collective_id=0, has_side_effects=True, vmem_limit_bytes=VMEM

time: 53.3 us -> 59 us (1.11)
  Pallas kernels: 52.1 us -> 57.9 us
    pallas_call x1, Pallas kernels: 52.1 us -> 57.9 us  [body(): pl.pallas_call(functools.partial(kernel, frames), out_shape=pltpu.VMEM(gr...]
where the time goes in v9:
time: 59 us; the launch traced here: 58.9 us
  Pallas kernels  57.9 us (98%)
  local copies, waits for them, and re-layouts  0.95 us (2%)
    pallas_call x1, Pallas kernels, body(): pl.pallas_call(functools.partial(kernel, frames), out_shape=pltpu.VMEM(gr...  57.9 us

profile of v9, /device:TPU:4, one launch (start us, length us, event | category | flops | bytes accessed | tf_op | source)
XLA Modules:
  0.0 58.9 jit_solution(6784164107865862659)
XLA Ops:
  0.0 57.9 %shard_map.55 = bf16[2,5,16,3072]{3,2,1,0:T(8,128)(2,1)S(1)} custom-call(s32[3,24]{1,0:T(4,128)} %bitcast.10, s32[1,32]{1,0:T(1,128)} %bitcast.11, bf16[2,5,16,3072]{3,2,1,0:T(8,128)(2,1)} %bitcast.7, bf16[2,5,16,3072]{3,2,1,0:T(8,128)(2,1)} %bitcast.8, bf16[2,5,16,3072]{3,2,1,0:T(8,128)(2,1)} %bitcast.9), custom_call_target="tpu_custom_call" | custom-call | tf_op jit(solution)/shard_map/pallas_call | solution.py:285
  57.9 0.9 %copy.7 = bf16[160,3072]{1,0:T(8,128)(2,1)} copy(bf16[160,3072]{1,0:T(8,128)(2,1)S(1)} %bitcast.6) | data formatting | bytes 1966080

commit v10 on v9

--- a/solution.py
+++ b/solution.py
@@ -13,7 +13,9 @@
 PAIRS = 5
 PIX = 16
 TW = 10
+TILE = 8
 LOCAL = 3
+BLOCK = 8 * ROWS * PIX
 VMEM = 62 * 2**20
 MESH = pl.DeviceIdType.MESH
 BIG = float(2**20)
@@ -21,7 +23,7 @@
 
 
 def query_features(pair, reach_h, reach_w):
-    shape = (8 * ROWS * PIX, DH)
+    shape = (BLOCK, DH)
     row = lax.broadcasted_iota(jnp.int32, shape, 0)
     col = lax.broadcasted_iota(jnp.int32, shape, 1)
     tile_y = row >> 7
@@ -37,11 +39,11 @@
     return jnp.where(inside, jnp.float32(0.0), jnp.float32(-BIG))
 
 
-def key_features(part, pair):
+def key_features(part, low, high):
     shape = (ROWS, PIX, DH)
     pix = lax.broadcasted_iota(jnp.int32, shape, 1)
     col = lax.broadcasted_iota(jnp.int32, shape, 2)
-    tile = (part // 4) * TW + 2 * pair + (pix >> 3)
+    tile = (part // 4) * TW + jnp.where(pix >= TILE, high, low)
     return jnp.where(col == tile, jnp.float32(1.0), jnp.float32(0.0)).astype(jnp.bfloat16)
 
 
@@ -51,7 +53,7 @@
 
 def kernel(
     frames, reach_hbm, valid_hbm, q_ref, k_ref, v_ref, out_ref,
-    qbuf, kvbuf, kfeat, obuf, reach_ref, valid_ref,
+    qbuf, kvbuf, kfeat, qfeat, upper, obuf, reach_ref, valid_ref,
     send_sem, in_sem, fwd_sem, halo_sem, out_send_sem, out_sem, small_sem, ready_sem,
 ):
     frame = lax.axis_index("frame")
@@ -129,7 +131,11 @@
 
     for part in range(8):
         for pair in range(PAIRS):
-            kfeat[part, :, pair] = key_features(part, pair)
+            kfeat[part, :, pair] = key_features(part, 2 * pair, 2 * pair + 1)
+        for pair in range(1, PAIRS - 1):
+            kfeat[part, :, PAIRS - 1 + pair] = key_features(part, 2 * pair + 2, 2 * pair - 1)
+    pix = lax.broadcasted_iota(jnp.int32, (PIX, DH), 0)
+    upper[...] = jnp.where(pix >= TILE, jnp.float32(1.0), jnp.float32(0.0)).astype(jnp.bfloat16)
 
     @pl.when(jnp.logical_not(has_prev))
     def _():
@@ -167,36 +173,53 @@
     live_prev = jnp.where(has_prev, valid_ref[0, jnp.maximum(frame - 1, 0)], 0)
     live_next = jnp.where(has_next, valid_ref[0, jnp.minimum(frame + 1, frames - 1)], 0)
 
-    def attend(head, pair):
+    def mask_rows(head, carry):
         row = group * LOCAL + head
-        reach_t = reach_ref[0, row]
-        base = query_features(pair, reach_ref[1, row], reach_ref[2, row])
-        near = reach_t >= 1
+        near = reach_ref[0, row] >= 1
         allowed = ((live_prev > 0) & near, live_own > 0, (live_next > 0) & near)
-        query = qbuf[head, :, :, pair].reshape(8 * ROWS * PIX, DH)
-        near_pairs = pl.ds(jnp.clip(pair - 1, 0, PAIRS - 3), 3)
-        count = 8 * ROWS * 3 * PIX
-        tiles = kfeat[:, :, near_pairs].reshape(count, DH)
+        for pair in range(PAIRS):
+            base = query_features(pair, reach_ref[1, row], reach_ref[2, row])
+            for slot in range(3):
+                level = jnp.where(allowed[slot], jnp.float32(0.0), jnp.float32(-BIG))
+                qfeat[head, pair, slot] = jnp.minimum(base, level).astype(jnp.bfloat16)
+        return carry
+
+    lax.fori_loop(0, LOCAL, mask_rows, 0)
+
+    def around(take, pair):
+        if pair in (0, PAIRS - 1):
+            both = (take(pair), take(abs(pair - 1)))
+        else:
+            is_upper = (upper[...] > 0)[None, None]
+            both = (take(pair), jnp.where(is_upper, take(pair - 1), take(pair + 1)))
+        return jnp.concatenate([block.reshape(BLOCK, DH) for block in both], axis=0)
+
+    def score(head, pair):
+        query = qbuf[head, :, :, pair].reshape(BLOCK, DH)
+        second = abs(pair - 1) if pair in (0, PAIRS - 1) else PAIRS - 1 + pair
+        tiles = jnp.concatenate(
+            [kfeat[:, :, at].reshape(BLOCK, DH) for at in (pair, second)], axis=0
+        )
         scores = []
         for slot in range(3):
-            features = jnp.minimum(
-                base, jnp.where(allowed[slot], jnp.float32(0.0), jnp.float32(-BIG))
-            ).astype(jnp.bfloat16)
-            keys = kvbuf[0, slot, head, :, :, near_pairs].reshape(count, DH)
+            keys = around(lambda at: kvbuf[0, slot, head, :, :, at], pair)
             scores.append(
                 lax.dot_general(
-                    jnp.concatenate([query, features], axis=1),
+                    jnp.concatenate([query, qfeat[head, pair, slot]], axis=1),
                     jnp.concatenate([keys, tiles], axis=1),
                     (((1,), (1,)), ((), ())),
                     preferred_element_type=jnp.float32,
                 )
             )
+        return scores
+
+    def mix(head, pair, scores):
         top = jnp.max(functools.reduce(jnp.maximum, scores), axis=1, keepdims=True)
-        ones = jnp.ones((count, DH), jnp.bfloat16)
+        ones = jnp.ones((2 * BLOCK, DH), jnp.bfloat16)
         mixed = None
         for slot in range(3):
             weights = jnp.exp2((scores[slot] - top) * SCALE).astype(jnp.bfloat16)
-            values = kvbuf[1, slot, head, :, :, near_pairs].reshape(count, DH)
+            values = around(lambda at: kvbuf[1, slot, head, :, :, at], pair)
             term = jnp.dot(
                 weights,
                 jnp.concatenate([values, ones], axis=1),
@@ -243,17 +266,13 @@
             def _():
                 forward(head, kv, 1).wait_recv()
 
-        def per_pair(pair, carry):
-            attend(head, pair)
-            for first, last in ((0, 3), (3, PAIRS)):
-
-                @pl.when(pair == last - 1)
-                def _():
-                    send_out(head, first, last)
-
-            return carry
-
-        lax.fori_loop(0, PAIRS, per_pair, 0)
+        scores = score(head, 0)
+        for pair in range(PAIRS):
+            following = score(head, pair + 1) if pair + 1 < PAIRS else None
+            mix(head, pair, scores)
+            scores = following
+            if pair in (2, PAIRS - 1):
+                send_out(head, 0 if pair == 2 else 3, pair + 1)
         return carry
 
     lax.fori_loop(0, LOCAL, per_head, 0)
@@ -290,7 +309,9 @@
             scratch_shapes=[
                 pltpu.VMEM((LOCAL,) + block, jnp.bfloat16),
                 pltpu.VMEM((2, 3, LOCAL) + block, jnp.bfloat16),
-                pltpu.VMEM(block, jnp.bfloat16),
+                pltpu.VMEM((8, ROWS, 2 * PAIRS - 2, PIX, DH), jnp.bfloat16),
+                pltpu.VMEM((LOCAL, PAIRS, 3, BLOCK, DH), jnp.bfloat16),
+                pltpu.VMEM((PIX, DH), jnp.bfloat16),
                 pltpu.VMEM((LOCAL,) + block, jnp.bfloat16),
                 pltpu.SMEM((3, head_reach.shape[0]), jnp.int32),
                 pltpu.SMEM((1, frames), jnp.int32),

time: 59 us -> 51 us (0.86); the launches traced: 58.9 us -> 50.2 us
  Pallas kernels: 57.9 us -> 49.3 us
    pallas_call x1, Pallas kernels: 57.9 us -> 49.3 us  [body(): pl.pallas_call(functools.partial(kernel, frames), out_shape=pltpu.VMEM(gr...]
where the time goes in v10:
time: 51 us; the launch traced here: 50.2 us
  Pallas kernels  49.3 us (97%)
  local copies, waits for them, and re-layouts  0.95 us (2%)
    pallas_call x1, Pallas kernels, body(): pl.pallas_call(functools.partial(kernel, frames), out_shape=pltpu.VMEM(gr...  49.3 us

profile of v10, /device:TPU:4, one launch (start us, length us, event | category | flops | bytes accessed | tf_op | source)
XLA Modules:
  0.0 50.2 jit_solution(14821543705962746087)
XLA Ops:
  0.0 49.3 %shard_map.55 = bf16[2,5,16,3072]{3,2,1,0:T(8,128)(2,1)S(1)} custom-call(s32[3,24]{1,0:T(4,128)} %bitcast.10, s32[1,32]{1,0:T(1,128)} %bitcast.11, bf16[2,5,16,3072]{3,2,1,0:T(8,128)(2,1)} %bitcast.7, bf16[2,5,16,3072]{3,2,1,0:T(8,128)(2,1)} %bitcast.8, bf16[2,5,16,3072]{3,2,1,0:T(8,128)(2,1)} %bitcast.9), custom_call_target="tpu_custom_call" | custom-call | tf_op jit(solution)/shard_map/pallas_call | solution.py:304
  49.3 0.9 %copy.7 = bf16[160,3072]{1,0:T(8,128)(2,1)} copy(bf16[160,3072]{1,0:T(8,128)(2,1)S(1)} %bitcast.6) | data formatting | bytes 1966080

commit v11 on v10

--- a/solution.py
+++ b/solution.py
@@ -69,9 +69,11 @@
     prev_id = {"frame": frame - 1, "head": swap(group, frame - 1)}
     next_id = {"frame": frame + 1, "head": swap(group, frame + 1)}
 
+    mirror = 1 - 2 * lax.rem(frame, 2)
+
     def peer(step):
-        part = lax.rem(me // 4 + step // 4, 2) * 4 + lax.rem(me + step, 4)
-        return part
+        across = lax.rem(me // 4 + step // 4, 2) * 4
+        return across + lax.rem(me + 4 + mirror * (step % 4), 4)
 
     barrier = pltpu.get_barrier_semaphore()
     for step in range(1, 8):
@@ -102,7 +104,7 @@
     def cols(of_group, head):
         return pl.ds(pl.multiple_of((of_group * LOCAL + head) * DH, DH), DH)
 
-    order = (5, 1, 4, 3, 6, 2, 7)
+    order = (5, 3, 4, 2, 7, 1, 6)
 
     def send(at, head):
         ref = (q_ref, k_ref, v_ref)[at]
@@ -271,8 +273,8 @@
             following = score(head, pair + 1) if pair + 1 < PAIRS else None
             mix(head, pair, scores)
             scores = following
-            if pair in (2, PAIRS - 1):
-                send_out(head, 0 if pair == 2 else 3, pair + 1)
+            if pair in (1, 3, PAIRS - 1):
+                send_out(head, pair // 2 * 2, pair + 1)
         return carry
 
     lax.fori_loop(0, LOCAL, per_head, 0)

time: 51 us -> 51.4 us (level)
  the two profiles are of different devices: /device:TPU:4 before, /device:TPU:1 now
where the time goes in v11:
time: 51.4 us; the launch traced here: 51.3 us
  Pallas kernels  50.3 us (98%)
  local copies, waits for them, and re-layouts  0.95 us (2%)
    pallas_call x1, Pallas kernels, body(): pl.pallas_call(functools.partial(kernel, frames), out_shape=pltpu.VMEM(gr...  50.3 us

profile of v11, /device:TPU:1, one launch (start us, length us, event | category | flops | bytes accessed | tf_op | source)
XLA Modules:
  0.0 51.3 jit_solution(6879453030197531538)
XLA Ops:
  0.0 50.3 %shard_map.55 = bf16[2,5,16,3072]{3,2,1,0:T(8,128)(2,1)S(1)} custom-call(s32[3,24]{1,0:T(4,128)} %bitcast.10, s32[1,32]{1,0:T(1,128)} %bitcast.11, bf16[2,5,16,3072]{3,2,1,0:T(8,128)(2,1)} %bitcast.7, bf16[2,5,16,3072]{3,2,1,0:T(8,128)(2,1)} %bitcast.8, bf16[2,5,16,3072]{3,2,1,0:T(8,128)(2,1)} %bitcast.9), custom_call_target="tpu_custom_call" | custom-call | tf_op jit(solution)/shard_map/pallas_call | solution.py:306
  50.4 0.9 %copy.7 = bf16[160,3072]{1,0:T(8,128)(2,1)} copy(bf16[160,3072]{1,0:T(8,128)(2,1)S(1)} %bitcast.6) | data formatting | bytes 1966080

commit v12 on v10

--- a/solution.py
+++ b/solution.py
@@ -81,23 +81,33 @@
 
     even = lax.rem(frame, 2) == 0
     odd = jnp.logical_not(even)
+    below_turn = odd & (frame == half - 1)
+    above_turn = even & (frame == half)
+    odd_to_next = odd & has_next & jnp.logical_not(below_turn)
+    even_to_prev = even & has_prev & jnp.logical_not(above_turn)
 
     def greet(sem, target):
         pl.semaphore_signal(sem, inc=1, device_id=target, device_id_type=MESH)
 
-    @pl.when(has_prev)
-    def _():
-        greet(barrier, prev_id)
-
-    @pl.when(even)
-    def _():
-        greet(barrier, next_id)
-
-    pl.semaphore_wait(barrier, 8 + jnp.where(odd & has_next, 1, 0))
-
-    @pl.when(odd & has_next)
-    def _():
-        greet(ready_sem, next_id)
+    def greet_or_answer(sem, to_mate, to_z, to_turn, mate, at_z, at_turn):
+        @pl.when(to_mate)
+        def _():
+            greet(sem, mate)
+
+        @pl.when(to_z)
+        def _():
+            greet(sem, at_z)
+
+        @pl.when(to_turn)
+        def _():
+            greet(sem, at_turn)
+
+    def count(*conditions):
+        return sum(jnp.where(condition, 1, 0) for condition in conditions)
+
+    greet_or_answer(barrier, odd, odd_to_next, above_turn, prev_id, next_id, prev_id)
+    pl.semaphore_wait(barrier, 7 + count(even, even_to_prev, below_turn))
+    greet_or_answer(ready_sem, even, even_to_prev, below_turn, next_id, prev_id, next_id)
 
     def cols(of_group, head):
         return pl.ds(pl.multiple_of((of_group * LOCAL + head) * DH, DH), DH)
@@ -244,9 +254,9 @@
             ).start()
         pltpu.make_async_copy(obuf.at[head, me, :, first:last], landing, out_sem).start()
 
-    @pl.when(even & has_prev)
+    @pl.when(odd | above_turn)
     def _():
-        pl.semaphore_wait(ready_sem, 1)
+        pl.semaphore_wait(ready_sem, count(odd, odd_to_next, above_turn))
 
     pass_on(0)
 

time: 51 us -> 50.6 us (level)
  no operation moved by 1% of the time
where the time goes in v12:
time: 50.6 us; the launch traced here: 49.7 us
  Pallas kernels  48.8 us (96%)
  local copies, waits for them, and re-layouts  0.95 us (2%)
    pallas_call x1, Pallas kernels, body(): pl.pallas_call(functools.partial(kernel, frames), out_shape=pltpu.VMEM(gr...  48.8 us

profile of v12, /device:TPU:4, one launch (start us, length us, event | category | flops | bytes accessed | tf_op | source)
XLA Modules:
  0.0 49.7 jit_solution(7804803383282131170)
XLA Ops:
  0.0 48.8 %shard_map.55 = bf16[2,5,16,3072]{3,2,1,0:T(8,128)(2,1)S(1)} custom-call(s32[3,24]{1,0:T(4,128)} %bitcast.10, s32[1,32]{1,0:T(1,128)} %bitcast.11, bf16[2,5,16,3072]{3,2,1,0:T(8,128)(2,1)} %bitcast.7, bf16[2,5,16,3072]{3,2,1,0:T(8,128)(2,1)} %bitcast.8, bf16[2,5,16,3072]{3,2,1,0:T(8,128)(2,1)} %bitcast.9), custom_call_target="tpu_custom_call" | custom-call | tf_op jit(solution)/shard_map/pallas_call | solution.py:314
  48.8 0.9 %copy.7 = bf16[160,3072]{1,0:T(8,128)(2,1)} copy(bf16[160,3072]{1,0:T(8,128)(2,1)S(1)} %bitcast.6) | data formatting | bytes 1966080

commit v13 on v12

--- a/solution.py
+++ b/solution.py
@@ -169,13 +169,23 @@
         for kv in range(2):
             wait_bytes(kvbuf.at[kv, 1, head], in_sem.at[kv + 1, head])
 
-            @pl.when(has_prev)
+            @pl.when(even & has_prev)
             def _():
                 forward(head, kv, 0).start()
 
-            @pl.when(has_next)
+            @pl.when(odd & has_next)
             def _():
                 forward(head, kv, 1).start()
+
+        for kv in range(2):
+
+            @pl.when(even)
+            def _():
+                forward(head, kv, 1).start()
+
+            @pl.when(odd)
+            def _():
+                forward(head, kv, 0).start()
 
     reach_copy.wait()
     valid_copy.wait()

time: 50.6 us -> 50.6 us (level)
  no operation moved by 1% of the time
where the time goes in v13:
time: 50.6 us; the launch traced here: 49.7 us
  Pallas kernels  48.8 us (96%)
  local copies, waits for them, and re-layouts  0.95 us (2%)
    pallas_call x1, Pallas kernels, body(): pl.pallas_call(functools.partial(kernel, frames), out_shape=pltpu.VMEM(gr...  48.8 us

profile of v13, /device:TPU:4, one launch (start us, length us, event | category | flops | bytes accessed | tf_op | source)
XLA Modules:
  0.0 49.7 jit_solution(3457458191033230335)
XLA Ops:
  0.0 48.8 %shard_map.55 = bf16[2,5,16,3072]{3,2,1,0:T(8,128)(2,1)S(1)} custom-call(s32[3,24]{1,0:T(4,128)} %bitcast.10, s32[1,32]{1,0:T(1,128)} %bitcast.11, bf16[2,5,16,3072]{3,2,1,0:T(8,128)(2,1)} %bitcast.7, bf16[2,5,16,3072]{3,2,1,0:T(8,128)(2,1)} %bitcast.8, bf16[2,5,16,3072]{3,2,1,0:T(8,128)(2,1)} %bitcast.9), custom_call_target="tpu_custom_call" | custom-call | tf_op jit(solution)/shard_map/pallas_call | solution.py:324
  48.8 0.9 %copy.7 = bf16[160,3072]{1,0:T(8,128)(2,1)} copy(bf16[160,3072]{1,0:T(8,128)(2,1)S(1)} %bitcast.6) | data formatting | bytes 1966080

commit v14 on v13

--- a/solution.py
+++ b/solution.py
@@ -271,9 +271,9 @@
     pass_on(0)
 
     def per_head(head, carry):
-        @pl.when(head < LOCAL - 1)
+        @pl.when(head == 1)
         def _():
-            pass_on(head + 1)
+            pass_on(2)
 
         wait_bytes(qbuf.at[head], in_sem.at[0, head])
         for kv in range(2):
@@ -291,6 +291,12 @@
             following = score(head, pair + 1) if pair + 1 < PAIRS else None
             mix(head, pair, scores)
             scores = following
+            if pair == 1:
+
+                @pl.when(head == 0)
+                def _():
+                    pass_on(1)
+
             if pair in (2, PAIRS - 1):
                 send_out(head, 0 if pair == 2 else 3, pair + 1)
         return carry

time: 50.6 us -> 50.4 us (level); the launches traced: 49.7 us -> 50.1 us
  no operation moved by 1% of the time
where the time goes in v14:
time: 50.4 us; the launch traced here: 50.1 us
  Pallas kernels  49.1 us (97%)
  local copies, waits for them, and re-layouts  0.95 us (2%)
    pallas_call x1, Pallas kernels, body(): pl.pallas_call(functools.partial(kernel, frames), out_shape=pltpu.VMEM(gr...  49.1 us

profile of v14, /device:TPU:4, one launch (start us, length us, event | category | flops | bytes accessed | tf_op | source)
XLA Modules:
  0.0 50.1 jit_solution(13724608434163943837)
XLA Ops:
  0.0 49.1 %shard_map.55 = bf16[2,5,16,3072]{3,2,1,0:T(8,128)(2,1)S(1)} custom-call(s32[3,24]{1,0:T(4,128)} %bitcast.10, s32[1,32]{1,0:T(1,128)} %bitcast.11, bf16[2,5,16,3072]{3,2,1,0:T(8,128)(2,1)} %bitcast.7, bf16[2,5,16,3072]{3,2,1,0:T(8,128)(2,1)} %bitcast.8, bf16[2,5,16,3072]{3,2,1,0:T(8,128)(2,1)} %bitcast.9), custom_call_target="tpu_custom_call" | custom-call | tf_op jit(solution)/shard_map/pallas_call | solution.py:330
  49.1 0.9 %copy.7 = bf16[160,3072]{1,0:T(8,128)(2,1)} copy(bf16[160,3072]{1,0:T(8,128)(2,1)S(1)} %bitcast.6) | data formatting | bytes 1966080
